TPU v7x, 128 devices: a whole 4x4x4 slice. The times are simulated.
128 devices in a mesh: lat: 8 (over x_lo, y), lon: 16 (over z, x_hi, core).
Axes of the slice: x: 4 (x_hi: 2, x_lo: 2; x = x_hi * 2 + x_lo), y: 4, z: 4, core: 2. Of those that a mesh axis runs over, the one named last changes fastest.
Arguments:
- records: bfloat16 [128, 128, 1024], P(('lat', 'lon')), may hold values from -6 to 6
- cell_ids: int32 [128, 128, 16], P(('lat', 'lon')), may hold values from 0 to 767
- counts: int32 [128, 128], P(('lat', 'lon')), may hold values from 0 to 16, as said below
- embed: bfloat16 [64, 256], replicated, may hold values from -0.75 to 0.75
- kernels: bfloat16 [3, 3, 3, 256, 256], replicated, may hold values from -0.125 to 0.125
- down: bfloat16 [2, 2, 256, 256], replicated, may hold values from -0.1875 to 0.1875
- cotangent: bfloat16 [64, 384, 256], P('lat', 'lon'), may hold values from -6 to 6
Outputs:
- coarse: bfloat16 [64, 384, 256], P('lat', 'lon')
- kernel_update: bfloat16 [3, 3, 3, 256, 256], replicated
- down_update: bfloat16 [2, 2, 256, 256], replicated
- embed_update: bfloat16 [64, 256], replicated
Inputs may be any that keep to these rules, and one draw needn't show every extreme that they name: counts[s, d] slots of the 16 from tile s to tile d are live, the first ones; the others carry records that no output reads. Every tile sends 16 records to itself, and some tile receives 16 from every tile.
All inputs are finite; a program needn't handle non-finite values.
Results may differ from a plain program's by a relative error of at most 0.015.
Values may be sent and summed in bfloat16 or wider, within the bound.
A program may use at most 128 MiB of HBM per device.

v0:
```python
import jax
import jax.numpy as jnp
from jax import lax
from jax.experimental import pallas as pl
from jax.experimental.pallas import tpu as pltpu
from jax.sharding import PartitionSpec as P

F32 = jnp.float32
BF16 = jnp.bfloat16
MESH = pl.DeviceIdType.MESH

ROWS, WIDE = 28, 64
PIECES = ((0, 1, 2), (3, 4), (5, 6, 7))
GROUPS = ((0, 3, 5), (1, 4, 6), (2, 7))
GROUP_OF = {u: g for g, us in enumerate(GROUPS) for u in us}
PLACE = {u: g * 3 + i for g, us in enumerate(GROUPS) for i, u in enumerate(us)}


def nn(a, b):
    return jnp.dot(a, b, preferred_element_type=F32)


def nt(a, b):
    return lax.dot_general(a, b, (((1,), (1,)), ((), ())), preferred_element_type=F32)


def body(
    values_ref, ids_ref, idst_ref, embed_ref, kern_ref, down_ref, cot_ref,
    coarse_ref, kup_ref, dup_ref, eup_ref,
    onehot, spread, mean, cpad, fine_e, fine_o, eo, up, x3, fac, dy3, dym, xt, xl, ybuf,
    grad, core_in, acc1, in1, acc2, in2, acc3, in3, gath,
    halo_s, halo_r, rs_s, rs_r, ag_s, ag_r,
):
    lat = lax.axis_index("lat")
    lon = lax.axis_index("lon")
    xx = lax.rem(lon // 2, 2) * 2 + lat // 4
    yy = lax.rem(lat, 4)
    zz = lon // 4
    core = lax.rem(lon, 2)
    pos = (xx, yy, zz)

    def at(axis, k):
        c = list(pos)
        c[axis] = lax.rem(c[axis] + k, 4)
        return (lax.rem(c[0], 2) * 4 + c[1], c[2] * 4 + (c[0] // 2) * 2 + core)

    other = (lat, lon + 1 - 2 * core)

    def side(dr, dc):
        return (lax.rem(lat + dr + 8, 8), lax.rem(lon + dc + 16, 16))

    sides = [(r, c) for r in (-1, 0, 1) for c in (-1, 0, 1) if (r, c) != (0, 0)]
    partners = [side(r, c) for r, c in sides] + [other]
    partners += [at(a, k) for a in range(3) for k in (1, 2, 3)]
    barrier = pltpu.get_barrier_semaphore()
    for who in partners:
        pl.semaphore_signal(barrier, inc=1, device_id=who, device_id_type=MESH)

    cpad[2:10, 8:32, :] = cot_ref[...].astype(F32)
    pl.semaphore_wait(barrier, len(partners))

    def span(step, rows, lead, cols, near):
        if step[0] == 0:
            r_src = r_dst = (lead, rows)
        elif step[0] < 0:
            r_src, r_dst = (lead, lead), (lead + rows, lead)
        else:
            r_src, r_dst = (rows, lead), (0, lead)
        if step[1] == 0:
            c_src = c_dst = (8, cols)
        elif step[1] < 0:
            c_src, c_dst = (8, 8), (8 + cols, 8)
        else:
            c_src, c_dst = (cols, 8), (0, 8)
        return r_src, c_src, r_dst, c_dst

    def halo(ref, rows, lead, cols, which):
        copies = []
        for n, step in enumerate(sides):
            (a, la), (b, lb), (c, lc), (d, ld) = span(step, rows, lead, cols, None)
            copies.append(
                pltpu.make_async_remote_copy(
                    src_ref=ref.at[pl.ds(a, la), pl.ds(b, lb), :],
                    dst_ref=ref.at[pl.ds(c, lc), pl.ds(d, ld), :],
                    send_sem=halo_s.at[which, n],
                    recv_sem=halo_r.at[which, n],
                    device_id=side(*step),
                    device_id_type=MESH,
                )
            )
        for c in copies:
            c.start()
        return copies

    cot_copies = halo(cpad, 8, 2, 24, 0)

    cells = lax.broadcasted_iota(jnp.int32, (384, 128), 0)
    low = lax.broadcasted_iota(jnp.int32, (128, 128), 1) < 64
    for k in range(16):
        idr = idst_ref[k : k + 1, :]
        row = (idr * 1366) >> 16
        place = (row >> 1) * 48 + (idr - row * 48)
        place = jnp.where(idr < 0, -1, place)
        onehot[:, k * 128 : (k + 1) * 128] = jnp.where(cells == place, 1.0, 0.0).astype(BF16)
        idc = ids_ref[:, k : k + 1]
        par = ((idc * 1366) >> 16) & 1
        even = jnp.where((idc >= 0) & (par == 0), 1.0, 0.0)
        odd = jnp.where((idc >= 0) & (par == 1), 1.0, 0.0)
        flag = jnp.where(low, even, odd)
        pair = values_ref[:, (k // 2) * 128 : (k // 2 + 1) * 128].astype(F32)
        swap = pltpu.roll(pair, 64, 1)
        both = jnp.where(low, pair, swap) if k % 2 == 0 else jnp.where(low, swap, pair)
        spread[k * 128 : (k + 1) * 128, 0:128] = (both * flag).astype(BF16)
        spread[k * 128 : (k + 1) * 128, 128:256] = flag.astype(BF16)
    sums = nn(onehot[...], spread[...])
    means = (sums[:, 0:128] / jnp.maximum(sums[:, 128:256], 1.0)).astype(BF16).astype(F32)
    mean[3:11, 8:56, :] = means.reshape(8, 48, 128)
    mean_copies = halo(mean, 8, 3, 48, 1)

    for c in cot_copies:
        c.wait_recv()
    fine_e[...] = jnp.zeros_like(fine_e)
    fine_o[...] = jnp.zeros_like(fine_o)
    coarse_cells = cpad[:, 4:36, :].reshape(384, 256)
    for h in range(2):
        part = coarse_cells[:, h * 128 : (h + 1) * 128]
        fine_e[h, pl.ds(0, 384, stride=2), :] = part
        fine_o[h, pl.ds(1, 384, stride=2), :] = part
    for h in range(2):
        eo[:, :, h * 128 : (h + 1) * 128] = fine_e[h].astype(BF16).reshape(12, WIDE, 128)
        eo[:, :, 256 + h * 128 : 256 + (h + 1) * 128] = fine_o[h].astype(BF16).reshape(12, WIDE, 128)
    for a in range(2):
        flat = eo[...].reshape(12 * WIDE, 512)
        top = nt(flat[:, 0:256], down_ref[a, 0]) + nt(flat[:, 256:512], down_ref[a, 1])
        top = top.reshape(12, WIDE, 256)
        for i in range(12):
            up[2 * i + a] = top[i]

    def inside(first, count):
        row = lax.broadcasted_iota(jnp.int32, (count, 1, 1), 0) + (lat * 16 - 6 + first)
        return jnp.where((row >= 0) & (row < 128), 1.0, 0.0)

    column = lax.broadcasted_iota(jnp.int32, (1, WIDE, 1), 1)
    in_tile = jnp.where((column >= 8) & (column < 56), 1.0, 0.0)

    def store3(ref, first, count, value, order):
        flat = value.reshape(count * WIDE, 256)
        prev = pltpu.roll(flat, 1, 0)
        nxt = pltpu.roll(flat, count * WIDE - 1, 0)
        parts = (prev, flat, nxt) if order > 0 else (nxt, flat, prev)
        for b, part in enumerate(parts):
            ref[first : first + count, :, b * 256 : (b + 1) * 256] = part.astype(BF16).reshape(count, WIDE, 256)

    def turn(ref_slice, count):
        return ref_slice.reshape(count * WIDE, 256).T

    for c in mean_copies:
        c.wait_recv()
    for first in (0, 7):
        lhs = mean[first : first + 7].reshape(7 * WIDE, 128).astype(BF16)
        zero = jnp.zeros((64, 256), BF16)
        for par in range(2):
            both = (embed_ref[...], zero) if par == 0 else (zero, embed_ref[...])
            x0 = nn(lhs, jnp.concatenate(both, 0)).reshape(7, WIDE, 256)
            row = lax.broadcasted_iota(jnp.int32, (7, 1, 1), 0) * 2 + (lat * 16 - 6 + 2 * first + par)
            x0 = x0 * jnp.where((row >= 0) & (row < 128), 1.0, 0.0)
            flat = x0.reshape(7 * WIDE, 256)
            parts = (pltpu.roll(flat, 1, 0), flat, pltpu.roll(flat, 7 * WIDE - 1, 0))
            for b, part in enumerate(parts):
                part = part.astype(BF16).reshape(7, WIDE, 256)
                for i in range(7):
                    x3[0, 2 * (first + i) + par, :, b * 256 : (b + 1) * 256] = part[i]

    for l in range(3):
        first, count = l + 1, 26 - 2 * l
        half = count // 2
        for start in (first, first + half):
            y = jnp.zeros((half * WIDE, 256), F32)
            for a in range(3):
                y = y + nn(
                    x3[l, start + a - 1 : start + a - 1 + half].reshape(half * WIDE, 768),
                    kern_ref[l, a].reshape(768, 256),
                )
            s = jax.nn.sigmoid(y)
            gain = (s * (1.0 + y * (1.0 - s))).reshape(half, WIDE, 256)
            keep = inside(start, half)
            fac[l, start : start + half] = gain * keep
            x = x3[l, start : start + half, :, 256:512].reshape(half * WIDE, 256).astype(F32)
            x = (x + y * s).reshape(half, WIDE, 256)
            if l < 2:
                store3(x3.at[l + 1], start, half, x * keep, 1)
            else:
                xl[start : start + half] = (x * in_tile).astype(BF16)

    sum0 = jnp.zeros((512, 256), F32)
    sum1 = jnp.zeros((512, 256), F32)
    last = xl[6:22].reshape(8, 2, WIDE, 256)
    rights = eo[2:10].reshape(512, 512)
    for a in range(2):
        piece = last[:, a].reshape(512, 256)
        sum0 = sum0 + nn(piece, down_ref[a, 0])
        sum1 = sum1 + nn(piece, down_ref[a, 1])
        g = nn(piece.T, rights).astype(BF16)
        for b in range(2):
            for e in range(2):
                grad[e, 2 * a + b] = g[:, b * 256 + e * 128 : b * 256 + (e + 1) * 128]
    total = sum0 + pltpu.roll(sum1, 511, 0)
    for h in range(2):
        ybuf[h] = total[:, h * 128 : (h + 1) * 128]
    for h in range(2):
        picked = ybuf[h, pl.ds(0, 256, stride=2), :].reshape(8, 32, 128)
        coarse_ref[:, :, h * 128 : (h + 1) * 128] = picked[:, 4:28].astype(BF16)

    copies = {}

    def send(key, src, dst, who, sems, index):
        c = pltpu.make_async_remote_copy(
            src_ref=src, dst_ref=dst, send_sem=sems[0].at[index], recv_sem=sems[1].at[index],
            device_id=who, device_id_type=MESH,
        )
        c.start()
        copies[key] = c

    rs = (rs_s, rs_r)
    ag = (ag_s, ag_r)

    def give_core(piece):
        b0, n = 4 * PIECES[piece][0], 4 * len(PIECES[piece])
        send(
            ("c", piece), grad.at[1 - core, pl.ds(b0, n)], core_in.at[pl.ds(b0, n)], other, rs, 72 + piece
        )

    def step1(piece):
        copies["c", piece].wait_recv()
        for u in PIECES[piece]:
            for p in range(4):
                acc1[4 * u + p] = (grad[core, 4 * u + p].astype(F32) + core_in[4 * u + p].astype(F32)).astype(BF16)
            axis = GROUP_OF[u]
            for k in (1, 2, 3):
                p = lax.rem(pos[axis] + k, 4)
                send(("1", u, k), acc1.at[4 * u + p], in1.at[u, k - 1], at(axis, k), rs, u * 9 + k - 1)

    def step2(u):
        axis, nxt = GROUP_OF[u], (GROUP_OF[u] + 1) % 3
        for k in (1, 2, 3):
            copies["1", u, k].wait_recv()
        s = acc1[4 * u + pos[axis]].astype(F32)
        for k in range(3):
            s = s + in1[u, k].astype(F32)
        acc2[u] = s.astype(BF16)
        for k in (1, 2, 3):
            p = lax.rem(pos[nxt] + k, 4)
            send(
                ("2", u, k), acc2.at[u, pl.ds(pl.multiple_of(p * 64, 64), 64)], in2.at[u, k - 1],
                at(nxt, k), rs, u * 9 + 3 + k - 1,
            )

    def step3(u):
        axis, nxt = (GROUP_OF[u] + 1) % 3, (GROUP_OF[u] + 2) % 3
        for k in (1, 2, 3):
            copies["2", u, k].wait_recv()
        s = acc2[u, pl.ds(pl.multiple_of(pos[axis] * 64, 64), 64), :].astype(F32)
        for k in range(3):
            s = s + in2[u, k].astype(F32)
        acc3[u] = s.astype(BF16)
        for k in (1, 2, 3):
            p = lax.rem(pos[nxt] + k, 4)
            send(
                ("3", u, k), acc3.at[u, pl.ds(pl.multiple_of(p * 16, 16), 16)], in3.at[u, k - 1],
                at(nxt, k), rs, u * 9 + 6 + k - 1,
            )

    def own_rows(g, level):
        p1, p2, p3 = pos[g], pos[(g + 1) % 3], pos[(g + 2) % 3]
        if level == 3:
            return p1, pl.ds(pl.multiple_of(p2 * 64 + p3 * 16, 16), 16)
        if level == 2:
            return p1, pl.ds(pl.multiple_of(p2 * 64, 64), 64)
        return p1, pl.ds(0, 256)

    def step4(u):
        axis = (GROUP_OF[u] + 2) % 3
        for k in (1, 2, 3):
            copies["3", u, k].wait_recv()
        s = acc3[u, pl.ds(pl.multiple_of(pos[axis] * 16, 16), 16), :].astype(F32)
        for k in range(3):
            s = s + in3[u, k].astype(F32)
        p1, rows = own_rows(GROUP_OF[u], 3)
        gath[core, p1, PLACE[u], rows, :] = s.astype(BF16)
        return jnp.sum(s * s)

    def back(l):
        lo, count = 5 - l, 18 + 2 * l
        half = count // 2
        for start in (lo, lo + half):
            rows = slice(start - lo, start - lo + half)
            d = up[start - 2 : start - 2 + half] * fac[l, start : start + half]
            store3(dy3, start, half, d, -1)
        d = dy3[6:22, :, 256:512].astype(F32) * in_tile
        store3(dym, 1, 16, d, -1)

    def weights(l):
        xt[...] = turn(x3[l, 5:23, :, 256:512], 18)
        block = 4 + 9 * (2 - l)
        for a in range(3):
            if a == 1:
                g = nn(xt[...], dym[...].reshape(18 * WIDE, 768))
            else:
                g = nn(xt[:, 64 * a : 64 * a + 1024], dym[1:17].reshape(16 * WIDE, 768))
            g = g.astype(BF16)
            for b in range(3):
                for e in range(2):
                    grad[e, block + 3 * a + b] = g[:, b * 256 + e * 128 : b * 256 + (e + 1) * 128]

    def spread_back(l):
        lo, count = 6 - l, 16 + 2 * l
        half = count // 2
        for start in (lo, lo + half):
            d = jnp.zeros((half * WIDE, 256), F32)
            for a in range(3):
                for b in range(3):
                    src = dy3[start + 1 - a : start + 1 - a + half, :, b * 256 : (b + 1) * 256]
                    d = d + nt(src.reshape(half * WIDE, 256), kern_ref[l, a, b])
            here = slice(start - 2, start - 2 + half)
            up[here] = up[here] + d.reshape(half, WIDE, 256)

    zero_row = jnp.zeros((WIDE, 768), BF16)
    dym[0] = zero_row
    dym[17] = zero_row
    back(2)
    weights(2)
    give_core(0)
    spread_back(2)
    step1(0)
    back(1)
    weights(1)
    give_core(1)
    for u in PIECES[0]:
        step2(u)
    spread_back(1)
    step1(1)
    back(0)
    weights(0)
    for u in PIECES[0]:
        step3(u)
    spread_back(0)
    for u in PIECES[1]:
        step2(u)
    squares = jnp.zeros((), F32)
    dx0 = (up[4:20] * in_tile).astype(BF16).reshape(8, 2, WIDE, 256)
    mt = mean[3:11].reshape(512, 128).T.astype(BF16)
    ge = nn(mt[0:64], dx0[:, 0].reshape(512, 256)) + nn(mt[64:128], dx0[:, 1].reshape(512, 256))
    for e in range(2):
        grad[e, 31] = jnp.zeros((256, 128), BF16)
        grad[e, 31, 0:64, :] = ge[:, e * 128 : (e + 1) * 128].astype(BF16)
    give_core(2)
    for u in PIECES[0]:
        squares = squares + step4(u)
    step1(2)
    for u in PIECES[1]:
        step3(u)
    for u in PIECES[2]:
        step2(u)
    for u in PIECES[1]:
        squares = squares + step4(u)
    for u in PIECES[2]:
        step3(u)
    for u in PIECES[2]:
        squares = squares + step4(u)

    p1, rows = own_rows(2, 3)
    full = jnp.full((8, 128), squares, F32)
    high = full.astype(BF16).astype(F32)
    gath[core, p1, 8, rows, :] = jnp.concatenate([high, full - high], 0).astype(BF16)

    for level in (3, 2, 1):
        for g in range(3):
            axis = (g + level - 1) % 3
            if level < 3:
                for k in (1, 2, 3):
                    copies["g", level + 1, g, k].wait_recv()
            p1, rows = own_rows(g, level)
            part = gath.at[core, p1, pl.ds(3 * g, 3), rows, :]
            for k in (1, 2, 3):
                send(("g", level, g, k), part, part, at(axis, k), ag, g * 9 + (3 - level) * 3 + k - 1)
    for g in range(3):
        part = gath.at[core, pos[g], pl.ds(3 * g, 3)]
        send(("h", g, 0), part, part, other, ag, 27 + g * 4)
    for k in (1, 2, 3):
        for g in range(3):
            copies["g", 1, g, k].wait_recv()
            part = gath.at[core, lax.rem(pos[g] + 4 - k, 4), pl.ds(3 * g, 3)]
            send(("h", g, k), part, part, other, ag, 27 + g * 4 + k)
    for g in range(3):
        for k in range(4):
            copies["h", g, k].wait_recv()

    stats = jnp.zeros((1, 128), F32)
    for e in range(2):
        for p in range(4):
            stats = stats + jnp.sum(gath[e, p, 8].astype(F32), axis=0, keepdims=True)
    entries = 31 * 65536 + 16384
    scale = 1.0 / jnp.sqrt(stats / (8.0 * entries) + 1e-06)
    for u in range(8):
        for p in range(4):
            block = 4 * u + p
            for e in range(2):
                v = (gath[e, p, PLACE[u]].astype(F32) * scale).astype(BF16)
                lanes = slice(e * 128, (e + 1) * 128)
                if block < 4:
                    dup_ref[block, :, lanes] = v
                elif block == 31:
                    eup_ref[:, lanes] = v[0:64]
                else:
                    l, tap = 2 - (block - 4) // 9, (block - 4) % 9
                    kup_ref[9 * l + tap, :, lanes] = v
    for c in cot_copies + mean_copies:
        c.wait_send()
    for c in copies.values():
        c.wait_send()


def on_device(records, cell_ids, counts, embed, kernels, down, cotangent):
    slot = jnp.arange(16, dtype=jnp.int32)[None, None, :]
    ids = jnp.where(slot < counts[:, :, None], cell_ids, -1)
    values = lax.all_to_all(records, ("lat", "lon"), split_axis=1, concat_axis=0, tiled=True).reshape(128, 1024)
    ids = lax.all_to_all(ids, ("lat", "lon"), split_axis=1, concat_axis=0, tiled=True).reshape(128, 16)
    vmem = pl.BlockSpec(memory_space=pltpu.VMEM)
    coarse, kup, dup, eup = pl.pallas_call(
        body,
        out_shape=(
            jax.ShapeDtypeStruct((8, 24, 256), BF16),
            jax.ShapeDtypeStruct((27, 256, 256), BF16),
            jax.ShapeDtypeStruct((4, 256, 256), BF16),
            jax.ShapeDtypeStruct((64, 256), BF16),
        ),
        in_specs=[vmem] * 7,
        out_specs=(vmem,) * 4,
        scratch_shapes=[
            pltpu.VMEM((384, 2048), BF16),
            pltpu.VMEM((2048, 256), BF16),
            pltpu.VMEM((14, WIDE, 128), F32),
            pltpu.VMEM((12, 40, 256), F32),
            pltpu.VMEM((2, 12 * WIDE, 128), F32),
            pltpu.VMEM((2, 12 * WIDE, 128), F32),
            pltpu.VMEM((12, WIDE, 512), BF16),
            pltpu.VMEM((24, WIDE, 256), F32),
            pltpu.VMEM((3, ROWS, WIDE, 768), BF16),
            pltpu.VMEM((3, ROWS, WIDE, 256), F32),
            pltpu.VMEM((ROWS, WIDE, 768), BF16),
            pltpu.VMEM((18, WIDE, 768), BF16),
            pltpu.VMEM((256, 18 * WIDE), BF16),
            pltpu.VMEM((ROWS, WIDE, 256), BF16),
            pltpu.VMEM((2, 512, 128), F32),
                pltpu.VMEM((2, 32, 256, 128), BF16),
            pltpu.VMEM((32, 256, 128), BF16),
            pltpu.VMEM((32, 256, 128), BF16),
            pltpu.VMEM((8, 3, 256, 128), BF16),
            pltpu.VMEM((8, 256, 128), BF16),
            pltpu.VMEM((8, 3, 64, 128), BF16),
            pltpu.VMEM((8, 64, 128), BF16),
            pltpu.VMEM((8, 3, 16, 128), BF16),
            pltpu.VMEM((2, 4, 9, 256, 128), BF16),
            pltpu.SemaphoreType.DMA((2, 8)),
            pltpu.SemaphoreType.DMA((2, 8)),
            pltpu.SemaphoreType.DMA((75,)),
            pltpu.SemaphoreType.DMA((75,)),
            pltpu.SemaphoreType.DMA((39,)),
            pltpu.SemaphoreType.DMA((39,)),
        ],
        compiler_params=pltpu.CompilerParams(
            collective_id=0, has_side_effects=True, vmem_limit_bytes=60 * 1024 * 1024
        ),
    )(values, ids, ids.T, embed, kernels, down, cotangent)
    return coarse, kup.reshape(3, 3, 3, 256, 256), dup.reshape(2, 2, 256, 256), eup


def solution(mesh):
    return jax.shard_map(
        on_device,
        mesh=mesh,
        in_specs=(
            P(("lat", "lon"), None, None),
            P(("lat", "lon"), None, None),
            P(("lat", "lon"), None),
            P(),
            P(),
            P(),
            P("lat", "lon", None),
        ),
        out_specs=(P("lat", "lon", None), P(), P(), P()),
        check_vma=False,
    )
```

profile of v0, /device:TPU:1, one launch (start us, length us, event | category | flops | bytes accessed | tf_op | source)
XLA Modules:
  0.0 126.4 jit_solution(13376785526051392295)
XLA Ops:
  0.6 0.7 fusion
  1.3 0.7 copy.25
  2.1 11.5 %all-to-all-start.1 = ((s32[1,128,16]{2,0,1:T(1,128)}), s32[1,128,16]{2,0,1:T(1,128)S(1)}, u32[]{:S(2)}, u32[]{:S(2)}) async-start(s32[1,128,16]{2,0,1:T(1,128)} %copy.25), calls=%async_computation.1 | async-start | bytes 131072 | tf_op jit(solution)/shard_map/all_to_all | solution.py:427
  13.6 1.4 %copy.33 = bf16[1,128,1024]{2,0,1:T(2,128)(2,1)S(1)} copy(bf16[1,128,1024]{2,1,0:T(8,128)(2,1)} %param.7) | data formatting | bytes 524288 | tf_op args[0]
  14.9 0.5 broadcast.26
  15.4 2.1 %reduce = bf16[128,1024]{1,0:T(8,128)(2,1)S(1)} reduce(bf16[128,1,1024]{2,1,0:T(2,128)(2,1)S(1)} %bitcast.18, bf16[]{:T(256)} %broadcast.26), dimensions={1}, to_apply=%bitcast.15.reduce_sub_computation | reduce | bytes 524290
  17.6 0.9 reshape.71
  18.5 4.6 %all-to-all-done.1 = s32[1,128,16]{2,0,1:T(1,128)S(1)} async-done(((s32[1,128,16]{2,0,1:T(1,128)}), s32[1,128,16]{2,0,1:T(1,128)S(1)}, u32[]{:S(2)}, u32[]{:S(2)}) %all-to-all-start.1) | async-done | bytes 8224 | tf_op jit(solution)/shard_map/all_to_all | solution.py:427
  23.1 0.0 copy-start
  23.1 5.1 %all-to-all-start = ((bf16[128,2,512]{2,1,0:T(2,128)(2,1)}), bf16[128,2,512]{2,1,0:T(2,128)(2,1)S(1)}, u32[]{:S(2)}, u32[]{:S(2)}) async-start(bf16[128,2,512]{2,1,0:T(2,128)(2,1)} %reshape.71), calls=%async_computation | async-start | bytes 524288 | tf_op jit(solution)/shard_map/all_to_all | solution.py:426
  28.3 0.7 copy.26
  28.9 10.5 %all-to-all-done = bf16[128,2,512]{2,1,0:T(2,128)(2,1)S(1)} async-done(((bf16[128,2,512]{2,1,0:T(2,128)(2,1)}), bf16[128,2,512]{2,1,0:T(2,128)(2,1)S(1)}, u32[]{:S(2)}, u32[]{:S(2)}) %all-to-all-start) | async-done | bytes 262176 | tf_op jit(solution)/shard_map/all_to_all | solution.py:426
  39.5 0.4 reshape.72
  39.9 0.8 copy.32
  40.7 0.0 copy-done
  40.7 78.5 %shard_map.105 = (bf16[8,24,256]{2,1,0:T(8,128)(2,1)}, bf16[27,256,256]{2,1,0:T(8,128)(2,1)}, bf16[4,256,256]{2,1,0:T(8,128)(2,1)}, bf16[64,256]{1,0:T(8,128)(2,1)}) custom-call(bf16[128,1024]{1,0:T(8,128)(2,1)} %bitcast.19, s32[128,16]{1,0:T(8,128)} %bitcast.20, s32[16,128]{1,0:T(8,128)} %bitcast.22, bf16[64,256]{1,0:T(8,128)(2,1)} %embed_ref.1, ...), custom_call_target="tpu_custom_call" | custom-call | tf_op jit(solution)/shard_map/pallas_call | solution.py:429
  119.2 1.5 %copy.38 = bf16[8,24,256]{2,1,0:T(8,128)(2,1)} copy(bf16[8,24,256]{2,1,0:T(8,128)(2,1)} %get-tuple-element.16) | data formatting | bytes 196608
  120.8 0.0 copy-start.1
  120.8 0.0 copy-start.2
  120.8 4.2 %copy.39 = bf16[3,3,3,256,256]{4,3,2,1,0:T(8,128)(2,1)} copy(bf16[3,3,3,256,256]{4,3,2,1,0:T(8,128)(2,1)} %bitcast.16) | data formatting | bytes 7077888
  125.0 0.0 copy-done.1
  125.0 0.8 copy.40
  125.8 0.0 copy-done.2
  125.8 0.6 copy.41
Async XLA Ops:
  2.1 21.1 %all-to-all-start.1 = ((s32[1,128,16]{2,0,1:T(1,128)}), s32[1,128,16]{2,0,1:T(1,128)S(1)}, u32[]{:S(2)}, u32[]{:S(2)}) async-start(s32[1,128,16]{2,0,1:T(1,128)} %copy.25), calls=%async_computation.1 | async-start | bytes 131072 | tf_op jit(solution)/shard_map/all_to_all | solution.py:427
  23.1 17.5 %copy-start = (s32[1,128,16]{2,0,1:T(1,128)}, s32[1,128,16]{2,0,1:T(1,128)S(1)}, u32[]{:S(2)}) copy-start(s32[1,128,16]{2,0,1:T(1,128)S(1)} %all-to-all-done.1) | copy-start | bytes 24580
  23.1 16.3 %all-to-all-start = ((bf16[128,2,512]{2,1,0:T(2,128)(2,1)}), bf16[128,2,512]{2,1,0:T(2,128)(2,1)S(1)}, u32[]{:S(2)}, u32[]{:S(2)}) async-start(bf16[128,2,512]{2,1,0:T(2,128)(2,1)} %reshape.71), calls=%async_computation | async-start | bytes 524288 | tf_op jit(solution)/shard_map/all_to_all | solution.py:426
  120.8 4.2 %copy-start.1 = (bf16[4,256,256]{2,1,0:T(8,128)(2,1)S(1)}, bf16[4,256,256]{2,1,0:T(8,128)(2,1)}, u32[]{:S(2)}) copy-start(bf16[4,256,256]{2,1,0:T(8,128)(2,1)} %get-tuple-element.10) | copy-start | bytes 1572868
  120.8 5.0 %copy-start.2 = (bf16[64,256]{1,0:T(8,128)(2,1)S(1)}, bf16[64,256]{1,0:T(8,128)(2,1)}, u32[]{:S(2)}) copy-start(bf16[64,256]{1,0:T(8,128)(2,1)} %get-tuple-element.19) | copy-start | bytes 98308
where the time goes:
time: 127 us; the launch traced here: 126 us
  Pallas kernels  78.5 us (62%)
  starting transfers between devices  16.6 us (13%)
  waiting for transfers between devices  15.2 us (12%)
  local copies, waits for them, and re-layouts  12.5 us (10%)
  other arithmetic  2.85 us (2%)
    pallas_call x1, Pallas kernels, on_device(): pl.pallas_call(body, out_shape=(jax.ShapeDtypeStruct((8, 24, 256), BF16),...  78.5 us
    all_to_all x1, starting transfers between devices, on_device(): lax.all_to_all(ids, ('lat', 'lon'), split_axis=1, concat_axis=0, tiled=True)  11.5 us
    unnamed x15, local copies, waits for them, and re-layouts  11.1 us
    all_to_all x1, waiting for transfers between devices, on_device(): lax.all_to_all(records, ('lat', 'lon'), split_axis=1, concat_axis=0, tile...  10.5 us
    all_to_all x1, starting transfers between devices, on_device(): lax.all_to_all(records, ('lat', 'lon'), split_axis=1, concat_axis=0, tile...  5.12 us
    all_to_all x1, waiting for transfers between devices, on_device(): lax.all_to_all(ids, ('lat', 'lon'), split_axis=1, concat_axis=0, tiled=True)  4.64 us
  transfers between devices with their start and end apart: 2, of which 2 were waited for; matrix products, arithmetic and copies ran while one was open for 4% of the time, Pallas kernels for 0%

commit v1 on v0

--- a/solution.py
+++ b/solution.py
@@ -11,7 +11,7 @@
 
 ROWS, WIDE = 28, 64
 PIECES = ((0, 1, 2), (3, 4), (5, 6, 7))
-GROUPS = ((0, 3, 5), (1, 4, 6), (2, 7))
+GROUPS = ((0, 3, 6), (1, 4, 7), (2, 5))
 GROUP_OF = {u: g for g, us in enumerate(GROUPS) for u in us}
 PLACE = {u: g * 3 + i for g, us in enumerate(GROUPS) for i, u in enumerate(us)}
 
@@ -25,12 +25,19 @@
 
 
 def body(
-    values_ref, ids_ref, idst_ref, embed_ref, kern_ref, down_ref, cot_ref,
-    coarse_ref, kup_ref, dup_ref, eup_ref,
+    records_ref, ids_ref, counts_ref, embed_ref, kern_hbm, down_hbm, cot_ref,
+    coarse_ref, gath, scale_ref,
+    kern_ref, down_ref, table, arr1, out2, in2,
     onehot, spread, mean, cpad, fine_e, fine_o, eo, up, x3, fac, dy3, dym, xt, xl, ybuf,
-    grad, core_in, acc1, in1, acc2, in2, acc3, in3, gath,
-    halo_s, halo_r, rs_s, rs_r, ag_s, ag_r,
+    grad, core_in, acc1, in1, acc2, in2r, acc3, in3,
+    load_s, d1_s, d1_r, d2_s, d2_r, halo_s, halo_r, rs_s, rs_r, ag_s, ag_r,
 ):
+    loads = [
+        pltpu.make_async_copy(kern_hbm, kern_ref, load_s.at[0]),
+        pltpu.make_async_copy(down_hbm, down_ref, load_s.at[1]),
+    ]
+    for c in loads:
+        c.start()
     lat = lax.axis_index("lat")
     lon = lax.axis_index("lon")
     xx = lax.rem(lon // 2, 2) * 2 + lat // 4
@@ -50,14 +57,57 @@
         return (lax.rem(lat + dr + 8, 8), lax.rem(lon + dc + 16, 16))
 
     sides = [(r, c) for r in (-1, 0, 1) for c in (-1, 0, 1) if (r, c) != (0, 0)]
-    partners = [side(r, c) for r, c in sides] + [other]
-    partners += [at(a, k) for a in range(3) for k in (1, 2, 3)]
+    partners = [(lax.rem(lat + k, 8), lon) for k in range(1, 8)]
+    partners += [(lat, lax.rem(lon + k, 16)) for k in range(1, 16)]
+    partners += [side(r, c) for r in (-1, 1) for c in (-1, 1)]
+    flip = lon + 2 - 4 * lax.rem(lon // 2, 2)
+    partners += [(lax.rem(lat + 4, 8), flip)]
     barrier = pltpu.get_barrier_semaphore()
     for who in partners:
         pl.semaphore_signal(barrier, inc=1, device_id=who, device_id_type=MESH)
 
+    live = jnp.broadcast_to(counts_ref[...].astype(F32), (128, 128)).T[:, 0:16]
+    slot = lax.broadcasted_iota(jnp.int32, (128, 16), 1).astype(F32)
+    cell = jnp.where(slot < live, ids_ref[...], 768)
+    kk = lax.broadcasted_iota(jnp.int32, (16, 128), 0)
+    ll = lax.broadcasted_iota(jnp.int32, (16, 128), 1)
+    lane = (kk >> 3) * 16 + (kk & 7)
+    digits = nn((cell >> 5).astype(F32).astype(BF16), jnp.where(ll == lane, 1.0, 0.0).astype(BF16))
+    digits = digits + nn((cell & 31).astype(F32).astype(BF16), jnp.where(ll == lane + 8, 1.0, 0.0).astype(BF16))
+    table[:, :, 0:1024] = records_ref[...].reshape(8, 16, 1024)
+    table[:, :, 1024:1152] = digits.astype(BF16).reshape(8, 16, 128)
     cpad[2:10, 8:32, :] = cot_ref[...].astype(F32)
     pl.semaphore_wait(barrier, len(partners))
+
+    def remote(src, dst, send_sem, recv_sem, who):
+        c = pltpu.make_async_remote_copy(
+            src_ref=src, dst_ref=dst, send_sem=send_sem, recv_sem=recv_sem, device_id=who, device_id_type=MESH
+        )
+        c.start()
+        return c
+
+    lat_copies = []
+    for k in range(1, 8):
+        p = lax.rem(lat + k, 8)
+        lat_copies.append(remote(table.at[p], arr1.at[lat], d1_s.at[k - 1], d1_r.at[k - 1], (p, lon)))
+    arr1[lat] = table[lat]
+    for c in lat_copies:
+        c.wait_recv()
+    flat = arr1[...].reshape(128, 1152)
+    rho = lax.broadcasted_iota(jnp.int32, (256, 128), 0)
+    came = lax.broadcasted_iota(jnp.int32, (256, 128), 1)
+    match = came == (rho & 7) * 16 + (rho >> 4)
+    halves = [jnp.where(match & (((rho >> 3) & 1) == h), 1.0, 0.0).astype(BF16) for h in range(2)]
+    second = pltpu.roll(flat[:, 1024:1152].astype(F32), 112, 1).astype(BF16)
+    moved = nn(halves[0], flat[:, 0:512]) + nn(halves[1], flat[:, 512:1024])
+    moved_ids = nn(halves[0], flat[:, 1024:1152]) + nn(halves[1], second)
+    out2[:, :, 0:512] = moved.astype(BF16).reshape(16, 16, 512)
+    out2[:, :, 512:640] = moved_ids.astype(BF16).reshape(16, 16, 128)
+    lon_copies = []
+    for k in range(1, 16):
+        q = lax.rem(lon + k, 16)
+        lon_copies.append(remote(out2.at[q], in2.at[lon], d2_s.at[k - 1], d2_r.at[k - 1], (lat, q)))
+    in2[lon] = out2[lon]
 
     def span(step, rows, lead, cols, near):
         if step[0] == 0:
@@ -94,29 +144,32 @@
 
     cot_copies = halo(cpad, 8, 2, 24, 0)
 
-    cells = lax.broadcasted_iota(jnp.int32, (384, 128), 0)
-    low = lax.broadcasted_iota(jnp.int32, (128, 128), 1) < 64
-    for k in range(16):
-        idr = idst_ref[k : k + 1, :]
-        row = (idr * 1366) >> 16
-        place = (row >> 1) * 48 + (idr - row * 48)
-        place = jnp.where(idr < 0, -1, place)
-        onehot[:, k * 128 : (k + 1) * 128] = jnp.where(cells == place, 1.0, 0.0).astype(BF16)
-        idc = ids_ref[:, k : k + 1]
-        par = ((idc * 1366) >> 16) & 1
-        even = jnp.where((idc >= 0) & (par == 0), 1.0, 0.0)
-        odd = jnp.where((idc >= 0) & (par == 1), 1.0, 0.0)
-        flag = jnp.where(low, even, odd)
-        pair = values_ref[:, (k // 2) * 128 : (k // 2 + 1) * 128].astype(F32)
+    for c in lon_copies:
+        c.wait_recv()
+    code = in2[:, :, 512:640].reshape(256, 128).astype(F32)
+    code = code * 32.0 + pltpu.roll(code, 120, 1)
+    odds = (((code.astype(jnp.int32) * 1366) >> 16) & 1).astype(F32)
+    idt = code.T[0:8].astype(jnp.int32)
+    rowt = (idt * 1366) >> 16
+    place = (rowt >> 1) * 48 + (idt - rowt * 48)
+    cells = lax.broadcasted_iota(jnp.int32, (384, 256), 0)
+    low = lax.broadcasted_iota(jnp.int32, (256, 128), 1) < 64
+    for k in range(8):
+        onehot[:, k * 256 : (k + 1) * 256] = jnp.where(cells == place[k : k + 1, :], 1.0, 0.0).astype(BF16)
+        odd = odds[:, k : k + 1]
+        flag = jnp.where(low, 1.0 - odd, odd)
+        pair = in2[:, :, (k // 2) * 128 : (k // 2 + 1) * 128].reshape(256, 128).astype(F32)
         swap = pltpu.roll(pair, 64, 1)
         both = jnp.where(low, pair, swap) if k % 2 == 0 else jnp.where(low, swap, pair)
-        spread[k * 128 : (k + 1) * 128, 0:128] = (both * flag).astype(BF16)
-        spread[k * 128 : (k + 1) * 128, 128:256] = flag.astype(BF16)
+        spread[k * 256 : (k + 1) * 256, 0:128] = (both * flag).astype(BF16)
+        spread[k * 256 : (k + 1) * 256, 128:256] = flag.astype(BF16)
     sums = nn(onehot[...], spread[...])
     means = (sums[:, 0:128] / jnp.maximum(sums[:, 128:256], 1.0)).astype(BF16).astype(F32)
     mean[3:11, 8:56, :] = means.reshape(8, 48, 128)
     mean_copies = halo(mean, 8, 3, 48, 1)
 
+    for c in loads:
+        c.wait()
     for c in cot_copies:
         c.wait_recv()
     fine_e[...] = jnp.zeros_like(fine_e)
@@ -251,7 +304,7 @@
         for k in (1, 2, 3):
             p = lax.rem(pos[nxt] + k, 4)
             send(
-                ("2", u, k), acc2.at[u, pl.ds(pl.multiple_of(p * 64, 64), 64)], in2.at[u, k - 1],
+                ("2", u, k), acc2.at[u, pl.ds(pl.multiple_of(p * 64, 64), 64)], in2r.at[u, k - 1],
                 at(nxt, k), rs, u * 9 + 3 + k - 1,
             )
 
@@ -261,7 +314,7 @@
             copies["2", u, k].wait_recv()
         s = acc2[u, pl.ds(pl.multiple_of(pos[axis] * 64, 64), 64), :].astype(F32)
         for k in range(3):
-            s = s + in2[u, k].astype(F32)
+            s = s + in2r[u, k].astype(F32)
         acc3[u] = s.astype(BF16)
         for k in (1, 2, 3):
             p = lax.rem(pos[nxt] + k, 4)
@@ -400,43 +453,73 @@
         for p in range(4):
             stats = stats + jnp.sum(gath[e, p, 8].astype(F32), axis=0, keepdims=True)
     entries = 31 * 65536 + 16384
-    scale = 1.0 / jnp.sqrt(stats / (8.0 * entries) + 1e-06)
+    scale_ref[...] = jnp.broadcast_to(1.0 / jnp.sqrt(stats / (8.0 * entries) + 1e-06), (8, 128))
+    for c in lat_copies + lon_copies + cot_copies + mean_copies:
+        c.wait_send()
+    for c in copies.values():
+        c.wait_send()
+
+
+def finish(gath_hbm, coarse_hbm, scale_ref, coarse_out, kup_out, dup_out, eup_out, gin, kup, dup, eup, in_s, out_s):
+    through = pltpu.make_async_copy(coarse_hbm, coarse_out, out_s.at[0])
+    through.start()
+    reads = []
     for u in range(8):
+        c = pltpu.make_async_copy(gath_hbm.at[:, :, PLACE[u]], gin.at[u], in_s.at[u])
+        c.start()
+        reads.append(c)
+    scale = scale_ref[0:1, :]
+    writes = [through]
+
+    def write(src, dst, index):
+        c = pltpu.make_async_copy(src, dst, out_s.at[index])
+        c.start()
+        writes.append(c)
+
+    for u in range(8):
+        reads[u].wait()
         for p in range(4):
             block = 4 * u + p
             for e in range(2):
-                v = (gath[e, p, PLACE[u]].astype(F32) * scale).astype(BF16)
                 lanes = slice(e * 128, (e + 1) * 128)
+                if block == 31:
+                    eup[:, lanes] = (gin[u, e, p, 0:64].astype(F32) * scale).astype(BF16)
+                    continue
+                v = (gin[u, e, p].astype(F32) * scale).astype(BF16)
                 if block < 4:
-                    dup_ref[block, :, lanes] = v
-                elif block == 31:
-                    eup_ref[:, lanes] = v[0:64]
+                    dup[block, :, lanes] = v
                 else:
-                    l, tap = 2 - (block - 4) // 9, (block - 4) % 9
-                    kup_ref[9 * l + tap, :, lanes] = v
-    for c in cot_copies + mean_copies:
-        c.wait_send()
-    for c in copies.values():
-        c.wait_send()
+                    kup[9 * (2 - (block - 4) // 9) + (block - 4) % 9, :, lanes] = v
+            if block == 3:
+                write(dup, dup_out, 1)
+            elif block == 31:
+                write(eup, eup_out, 2)
+            elif (block - 4) % 9 == 8:
+                l = 2 - (block - 4) // 9
+                write(kup.at[pl.ds(9 * l, 9)], kup_out.at[pl.ds(9 * l, 9)], 3 + l)
+    for c in writes:
+        c.wait()
 
 
 def on_device(records, cell_ids, counts, embed, kernels, down, cotangent):
-    slot = jnp.arange(16, dtype=jnp.int32)[None, None, :]
-    ids = jnp.where(slot < counts[:, :, None], cell_ids, -1)
-    values = lax.all_to_all(records, ("lat", "lon"), split_axis=1, concat_axis=0, tiled=True).reshape(128, 1024)
-    ids = lax.all_to_all(ids, ("lat", "lon"), split_axis=1, concat_axis=0, tiled=True).reshape(128, 16)
     vmem = pl.BlockSpec(memory_space=pltpu.VMEM)
-    coarse, kup, dup, eup = pl.pallas_call(
+    hbm = pl.BlockSpec(memory_space=pl.ANY)
+    coarse, gath, scale = pl.pallas_call(
         body,
         out_shape=(
             jax.ShapeDtypeStruct((8, 24, 256), BF16),
-            jax.ShapeDtypeStruct((27, 256, 256), BF16),
-            jax.ShapeDtypeStruct((4, 256, 256), BF16),
-            jax.ShapeDtypeStruct((64, 256), BF16),
+            jax.ShapeDtypeStruct((2, 4, 9, 256, 128), BF16),
+            jax.ShapeDtypeStruct((8, 128), F32),
         ),
-        in_specs=[vmem] * 7,
-        out_specs=(vmem,) * 4,
+        in_specs=[vmem, vmem, vmem, vmem, hbm, hbm, vmem],
+        out_specs=(vmem,) * 3,
         scratch_shapes=[
+            pltpu.VMEM((3, 3, 3, 256, 256), BF16),
+            pltpu.VMEM((2, 2, 256, 256), BF16),
+            pltpu.VMEM((8, 16, 1152), BF16),
+            pltpu.VMEM((8, 16, 1152), BF16),
+            pltpu.VMEM((16, 16, 640), BF16),
+            pltpu.VMEM((16, 16, 640), BF16),
             pltpu.VMEM((384, 2048), BF16),
             pltpu.VMEM((2048, 256), BF16),
             pltpu.VMEM((14, WIDE, 128), F32),
@@ -460,7 +543,11 @@
             pltpu.VMEM((8, 3, 64, 128), BF16),
             pltpu.VMEM((8, 64, 128), BF16),
             pltpu.VMEM((8, 3, 16, 128), BF16),
-            pltpu.VMEM((2, 4, 9, 256, 128), BF16),
+            pltpu.SemaphoreType.DMA((2,)),
+            pltpu.SemaphoreType.DMA((7,)),
+            pltpu.SemaphoreType.DMA((7,)),
+            pltpu.SemaphoreType.DMA((15,)),
+            pltpu.SemaphoreType.DMA((15,)),
             pltpu.SemaphoreType.DMA((2, 8)),
             pltpu.SemaphoreType.DMA((2, 8)),
             pltpu.SemaphoreType.DMA((75,)),
@@ -471,7 +558,27 @@
         compiler_params=pltpu.CompilerParams(
             collective_id=0, has_side_effects=True, vmem_limit_bytes=60 * 1024 * 1024
         ),
-    )(values, ids, ids.T, embed, kernels, down, cotangent)
+    )(records.reshape(128, 1024), cell_ids.reshape(128, 16), counts, embed, kernels, down, cotangent)
+    coarse, kup, dup, eup = pl.pallas_call(
+        finish,
+        out_shape=(
+            jax.ShapeDtypeStruct((8, 24, 256), BF16),
+            jax.ShapeDtypeStruct((27, 256, 256), BF16),
+            jax.ShapeDtypeStruct((4, 256, 256), BF16),
+            jax.ShapeDtypeStruct((64, 256), BF16),
+        ),
+        in_specs=[hbm, hbm, vmem],
+        out_specs=(hbm,) * 4,
+        scratch_shapes=[
+            pltpu.VMEM((8, 2, 4, 256, 128), BF16),
+            pltpu.VMEM((27, 256, 256), BF16),
+            pltpu.VMEM((4, 256, 256), BF16),
+            pltpu.VMEM((64, 256), BF16),
+            pltpu.SemaphoreType.DMA((8,)),
+            pltpu.SemaphoreType.DMA((6,)),
+        ],
+        compiler_params=pltpu.CompilerParams(vmem_limit_bytes=24 * 1024 * 1024),
+    )(gath, coarse, scale)
     return coarse, kup.reshape(3, 3, 3, 256, 256), dup.reshape(2, 2, 256, 256), eup
 
 

time: 127 us -> 105 us (0.83)
  Pallas kernels: 78.5 us -> 99.1 us
  starting transfers between devices: 16.6 us -> 0 us
  waiting for transfers between devices: 15.2 us -> 0 us
  local copies, waits for them, and re-layouts: 12.5 us -> 5.32 us
  other arithmetic: 2.85 us -> 0 us
    pallas_call x1, Pallas kernels: 78.5 us -> 96.5 us  [on_device(): pl.pallas_call(body, out_shape=(jax.ShapeDtypeStruct((8, 24, 256), BF16),...]
    all_to_all x2 -> x0, starting transfers between devices: 16.6 us -> none  [the longest x1 11.5 us: on_device(): lax.all_to_all(ids, ('lat', 'lon'), split_axis=1, concat_axis=0, tiled=True)]
    all_to_all x2 -> x0, waiting for transfers between devices: 15.2 us -> none  [the longest x1 10.5 us: on_device(): lax.all_to_all(records, ('lat', 'lon'), split_axis=1, concat_axis=0, tile...]
    unnamed x15 -> x7, local copies, waits for them, and re-layouts: 11.1 us -> 5.32 us
    pallas_call x0 -> x1, Pallas kernels: none -> 2.54 us  [on_device(): pl.pallas_call(finish, out_shape=(jax.ShapeDtypeStruct((8, 24, 256), BF16...]
    unnamed x1 -> x0, other arithmetic: 2.15 us -> none
  transfers between devices with their start and end apart: 2 -> 0, of which waited for: 2 -> 0; matrix products, arithmetic and copies ran while one was open for 4% -> 0% of each run, Pallas kernels for 0% -> 0%
where the time goes in v1:
time: 105 us
  Pallas kernels  99.1 us (94%)
  local copies, waits for them, and re-layouts  5.32 us (5%)
    pallas_call x1, Pallas kernels, on_device(): pl.pallas_call(body, out_shape=(jax.ShapeDtypeStruct((8, 24, 256), BF16),...  96.5 us
    unnamed x7, local copies, waits for them, and re-layouts  5.32 us
    pallas_call x1, Pallas kernels, on_device(): pl.pallas_call(finish, out_shape=(jax.ShapeDtypeStruct((8, 24, 256), BF16...  2.54 us

profile of v1, /device:TPU:1, one launch (start us, length us, event | category | flops | bytes accessed | tf_op | source)
XLA Modules:
  0.0 105.2 jit_solution(12153177289900987268)
XLA Ops:
  0.6 1.4 %copy.11 = s32[1,128,16]{2,1,0:T(8,128)} copy(s32[1,128,16]{1,2,0:T(8,128)} %param.8) | data formatting | bytes 16384 | tf_op args[1]
  2.1 96.5 %shard_map.102 = (bf16[8,24,256]{2,1,0:T(8,128)(2,1)}, bf16[2,4,9,256,128]{4,3,2,1,0:T(8,128)(2,1)}, f32[8,128]{1,0:T(8,128)}) custom-call(bf16[128,1024]{1,0:T(8,128)(2,1)} %bitcast.5, s32[128,16]{1,0:T(8,128)} %bitcast.4, s32[1,128]{1,0:T(1,128)} %counts_ref.1, bf16[64,256]{1,0:T(8,128)(2,1)} %embed_ref.1, bf16[3,3,3,256,256]{4,3,2,1,0:T(8,128)(2,1)} %kern_hbm.1, ...), custom_call_target="tpu_custom_call" | custom-call | tf_op jit(solution)/shard_map/pallas_call | solution.py:507
  98.6 0.0 copy-start
  98.6 2.3 %copy-done = bf16[2,4,9,256,128]{4,3,2,1,0:T(8,128)(2,1)S(1)} copy-done((bf16[2,4,9,256,128]{4,3,2,1,0:T(8,128)(2,1)S(1)}, bf16[2,4,9,256,128]{4,3,2,1,0:T(8,128)(2,1)}, u32[]{:S(2)}) %copy-start) | copy-done | bytes 4718616
  100.9 0.0 copy-start.1
  100.9 0.9 copy-done.1
  101.8 0.0 copy-start.2
  101.8 0.7 copy-done.2
  102.5 2.5 %shard_map.103 = (bf16[8,24,256]{2,1,0:T(8,128)(2,1)}, bf16[27,256,256]{2,1,0:T(8,128)(2,1)}, bf16[4,256,256]{2,1,0:T(8,128)(2,1)}, bf16[64,256]{1,0:T(8,128)(2,1)}) custom-call(bf16[2,4,9,256,128]{4,3,2,1,0:T(8,128)(2,1)S(1)} %copy-done, bf16[8,24,256]{2,1,0:T(8,128)(2,1)S(1)} %copy-done.1, f32[8,128]{1,0:T(8,128)S(1)} %copy-done.2), custom_call_target="tpu_custom_call" | custom-call | tf_op jit(solution)/shard_map/pallas_call | solution.py:562
Async XLA Ops:
  98.6 2.3 %copy-start = (bf16[2,4,9,256,128]{4,3,2,1,0:T(8,128)(2,1)S(1)}, bf16[2,4,9,256,128]{4,3,2,1,0:T(8,128)(2,1)}, u32[]{:S(2)}) copy-start(bf16[2,4,9,256,128]{4,3,2,1,0:T(8,128)(2,1)} %get-tuple-element.11.gath_hbm) | copy-start | bytes 14155780
  100.9 0.9 copy-start.1
  101.8 0.7 copy-start.2

commit v2 on v1

--- a/solution.py
+++ b/solution.py
@@ -10,10 +10,8 @@
 MESH = pl.DeviceIdType.MESH
 
 ROWS, WIDE = 28, 64
-PIECES = ((0, 1, 2), (3, 4), (5, 6, 7))
-GROUPS = ((0, 3, 6), (1, 4, 7), (2, 5))
-GROUP_OF = {u: g for g, us in enumerate(GROUPS) for u in us}
-PLACE = {u: g * 3 + i for g, us in enumerate(GROUPS) for i, u in enumerate(us)}
+PIECES = ((0,), (1, 2), (3, 4), (5, 6), (7,))
+PLANE = [(kb, kc) for kb in range(4) for kc in range(4) if (kb, kc) != (0, 0)]
 
 
 def nn(a, b):
@@ -26,11 +24,11 @@
 
 def body(
     records_ref, ids_ref, counts_ref, embed_ref, kern_hbm, down_hbm, cot_ref,
-    coarse_ref, gath, scale_ref,
+    coarse_ref, gath_hbm, scale_ref,
     kern_ref, down_ref, table, arr1, out2, in2,
     onehot, spread, mean, cpad, fine_e, fine_o, eo, up, x3, fac, dy3, dym, xt, xl, ybuf,
-    grad, core_in, acc1, in1, acc2, in2r, acc3, in3,
-    load_s, d1_s, d1_r, d2_s, d2_r, halo_s, halo_r, rs_s, rs_r, ag_s, ag_r,
+    grad, core_in, acc1, in1, acc2, in2r, gath,
+    load_s, d1_s, d1_r, d2_s, d2_r, halo_s, halo_r, sum_s, sum_r, out_s,
 ):
     loads = [
         pltpu.make_async_copy(kern_hbm, kern_ref, load_s.at[0]),
@@ -46,10 +44,16 @@
     core = lax.rem(lon, 2)
     pos = (xx, yy, zz)
 
-    def at(axis, k):
-        c = list(pos)
-        c[axis] = lax.rem(c[axis] + k, 4)
+    def by(offsets):
+        c = [lax.rem(p + o, 4) for p, o in zip(pos, offsets)]
         return (lax.rem(c[0], 2) * 4 + c[1], c[2] * 4 + (c[0] // 2) * 2 + core)
+
+    def along(axis, k):
+        return by([k if i == axis else 0 for i in range(3)])
+
+    def across(axis, kb, kc):
+        b, c = (axis + 1) % 3, (axis + 2) % 3
+        return by([kb if i == b else kc if i == c else 0 for i in range(3)])
 
     other = (lat, lon + 1 - 2 * core)
 
@@ -57,23 +61,22 @@
         return (lax.rem(lat + dr + 8, 8), lax.rem(lon + dc + 16, 16))
 
     sides = [(r, c) for r in (-1, 0, 1) for c in (-1, 0, 1) if (r, c) != (0, 0)]
-    partners = [(lax.rem(lat + k, 8), lon) for k in range(1, 8)]
-    partners += [(lat, lax.rem(lon + k, 16)) for k in range(1, 16)]
+    partners = [by((dx, dy, 0)) for dx, dy in PLANE]
+    partners += [by((0, dy, dz)) for dy in range(4) for dz in (1, 2, 3)]
+    partners += [by((dx, 0, dz)) for dx in (1, 2, 3) for dz in (1, 2, 3)]
+    partners += [(lat, lax.rem(lon + k, 16)) for k in range(1, 16, 2)]
     partners += [side(r, c) for r in (-1, 1) for c in (-1, 1)]
-    flip = lon + 2 - 4 * lax.rem(lon // 2, 2)
-    partners += [(lax.rem(lat + 4, 8), flip)]
     barrier = pltpu.get_barrier_semaphore()
     for who in partners:
         pl.semaphore_signal(barrier, inc=1, device_id=who, device_id_type=MESH)
 
-    live = jnp.broadcast_to(counts_ref[...].astype(F32), (128, 128)).T[:, 0:16]
-    slot = lax.broadcasted_iota(jnp.int32, (128, 16), 1).astype(F32)
-    cell = jnp.where(slot < live, ids_ref[...], 768)
-    kk = lax.broadcasted_iota(jnp.int32, (16, 128), 0)
-    ll = lax.broadcasted_iota(jnp.int32, (16, 128), 1)
+    cell = jnp.where(lax.broadcasted_iota(jnp.int32, (16, 128), 0) < counts_ref[...], ids_ref[...], 768)
+    kk = lax.broadcasted_iota(jnp.int32, (128, 16), 1)
+    ll = lax.broadcasted_iota(jnp.int32, (128, 16), 0)
     lane = (kk >> 3) * 16 + (kk & 7)
-    digits = nn((cell >> 5).astype(F32).astype(BF16), jnp.where(ll == lane, 1.0, 0.0).astype(BF16))
-    digits = digits + nn((cell & 31).astype(F32).astype(BF16), jnp.where(ll == lane + 8, 1.0, 0.0).astype(BF16))
+    digits = nn(jnp.where(ll == lane, 1.0, 0.0).astype(BF16), (cell >> 5).astype(F32).astype(BF16))
+    digits = digits + nn(jnp.where(ll == lane + 8, 1.0, 0.0).astype(BF16), (cell & 31).astype(F32).astype(BF16))
+    digits = digits.T
     table[:, :, 0:1024] = records_ref[...].reshape(8, 16, 1024)
     table[:, :, 1024:1152] = digits.astype(BF16).reshape(8, 16, 128)
     cpad[2:10, 8:32, :] = cot_ref[...].astype(F32)
@@ -265,82 +268,75 @@
         coarse_ref[:, :, h * 128 : (h + 1) * 128] = picked[:, 4:28].astype(BF16)
 
     copies = {}
-
-    def send(key, src, dst, who, sems, index):
-        c = pltpu.make_async_remote_copy(
-            src_ref=src, dst_ref=dst, send_sem=sems[0].at[index], recv_sem=sems[1].at[index],
-            device_id=who, device_id_type=MESH,
-        )
-        c.start()
-        copies[key] = c
-
-    rs = (rs_s, rs_r)
-    ag = (ag_s, ag_r)
-
-    def give_core(piece):
+    stores = []
+
+    def send(key, src, dst, who, index):
+        copies[key] = remote(src, dst, sum_s.at[index], sum_r.at[index], who)
+
+    def rs_core(piece):
         b0, n = 4 * PIECES[piece][0], 4 * len(PIECES[piece])
-        send(
-            ("c", piece), grad.at[1 - core, pl.ds(b0, n)], core_in.at[pl.ds(b0, n)], other, rs, 72 + piece
-        )
-
-    def step1(piece):
+        send(("c", piece), grad.at[1 - core, pl.ds(b0, n)], core_in.at[pl.ds(b0, n)], other, 37 * 8 + piece)
+
+    def rs_axis(piece):
         copies["c", piece].wait_recv()
         for u in PIECES[piece]:
             for p in range(4):
                 acc1[4 * u + p] = (grad[core, 4 * u + p].astype(F32) + core_in[4 * u + p].astype(F32)).astype(BF16)
-            axis = GROUP_OF[u]
             for k in (1, 2, 3):
-                p = lax.rem(pos[axis] + k, 4)
-                send(("1", u, k), acc1.at[4 * u + p], in1.at[u, k - 1], at(axis, k), rs, u * 9 + k - 1)
-
-    def step2(u):
-        axis, nxt = GROUP_OF[u], (GROUP_OF[u] + 1) % 3
+                p = lax.rem(pos[u % 3] + k, 4)
+                send(("a", u, k), acc1.at[4 * u + p], in1.at[u, k - 1], along(u % 3, k), u * 37 + k - 1)
+
+    def rs_plane(u):
+        axis = u % 3
         for k in (1, 2, 3):
-            copies["1", u, k].wait_recv()
+            copies["a", u, k].wait_recv()
         s = acc1[4 * u + pos[axis]].astype(F32)
         for k in range(3):
             s = s + in1[u, k].astype(F32)
         acc2[u] = s.astype(BF16)
+        for i, (kb, kc) in enumerate(PLANE):
+            row = lax.rem(pos[(axis + 1) % 3] + kb, 4) * 64 + lax.rem(pos[(axis + 2) % 3] + kc, 4) * 16
+            src = acc2.at[u, pl.ds(pl.multiple_of(row, 16), 16)]
+            send(("b", u, i), src, in2r.at[u, i], across(axis, kb, kc), u * 37 + 3 + i)
+
+    def ag_plane(u):
+        axis = u % 3
+        for i in range(15):
+            copies["b", u, i].wait_recv()
+        rows = pl.ds(pl.multiple_of(pos[(axis + 1) % 3] * 64 + pos[(axis + 2) % 3] * 16, 16), 16)
+        s = acc2[u, rows, :].astype(F32)
+        for i in range(15):
+            s = s + in2r[u, i].astype(F32)
+        part = gath.at[u, core, pos[axis], rows, :]
+        gath[u, core, pos[axis], rows, :] = s.astype(BF16)
+        for i, (kb, kc) in enumerate(PLANE):
+            send(("p", u, i), part, part, across(axis, kb, kc), u * 37 + 18 + i)
+
+    def ag_axis(u):
+        axis = u % 3
+        for i in range(15):
+            copies["p", u, i].wait_recv()
+        part = gath.at[u, core, pos[axis]]
         for k in (1, 2, 3):
-            p = lax.rem(pos[nxt] + k, 4)
-            send(
-                ("2", u, k), acc2.at[u, pl.ds(pl.multiple_of(p * 64, 64), 64)], in2r.at[u, k - 1],
-                at(nxt, k), rs, u * 9 + 3 + k - 1,
-            )
-
-    def step3(u):
-        axis, nxt = (GROUP_OF[u] + 1) % 3, (GROUP_OF[u] + 2) % 3
+            send(("g", u, k), part, part, along(axis, k), u * 37 + 33 + k - 1)
+
+    def ag_core(u):
         for k in (1, 2, 3):
-            copies["2", u, k].wait_recv()
-        s = acc2[u, pl.ds(pl.multiple_of(pos[axis] * 64, 64), 64), :].astype(F32)
-        for k in range(3):
-            s = s + in2r[u, k].astype(F32)
-        acc3[u] = s.astype(BF16)
-        for k in (1, 2, 3):
-            p = lax.rem(pos[nxt] + k, 4)
-            send(
-                ("3", u, k), acc3.at[u, pl.ds(pl.multiple_of(p * 16, 16), 16)], in3.at[u, k - 1],
-                at(nxt, k), rs, u * 9 + 6 + k - 1,
-            )
-
-    def own_rows(g, level):
-        p1, p2, p3 = pos[g], pos[(g + 1) % 3], pos[(g + 2) % 3]
-        if level == 3:
-            return p1, pl.ds(pl.multiple_of(p2 * 64 + p3 * 16, 16), 16)
-        if level == 2:
-            return p1, pl.ds(pl.multiple_of(p2 * 64, 64), 64)
-        return p1, pl.ds(0, 256)
-
-    def step4(u):
-        axis = (GROUP_OF[u] + 2) % 3
-        for k in (1, 2, 3):
-            copies["3", u, k].wait_recv()
-        s = acc3[u, pl.ds(pl.multiple_of(pos[axis] * 16, 16), 16), :].astype(F32)
-        for k in range(3):
-            s = s + in3[u, k].astype(F32)
-        p1, rows = own_rows(GROUP_OF[u], 3)
-        gath[core, p1, PLACE[u], rows, :] = s.astype(BF16)
-        return jnp.sum(s * s)
+            copies["g", u, k].wait_recv()
+        part = gath.at[u, core]
+        send(("h", u), part, part, other, u * 37 + 36)
+
+    def square(u):
+        copies["h", u].wait_recv()
+        c = pltpu.make_async_copy(gath.at[u], gath_hbm.at[u], out_s.at[u])
+        c.start()
+        stores.append(c)
+        total = jnp.zeros((8, 128), F32)
+        for e in range(2):
+            for p in range(4):
+                v = gath[u, e, p].astype(F32)
+                total = total + jnp.sum((v * v).reshape(32, 8, 128), axis=0)
+        return total
 
     def back(l):
         lo, count = 5 - l, 18 + 2 * l
@@ -380,84 +376,75 @@
     zero_row = jnp.zeros((WIDE, 768), BF16)
     dym[0] = zero_row
     dym[17] = zero_row
+    def each(step, piece):
+        for u in PIECES[piece]:
+            step(u)
+
+    def sent(kinds):
+        for key in [key for key in copies if key[0] in kinds]:
+            copies.pop(key).wait_send()
+
+    rs_core(0)
     back(2)
+    rs_axis(0)
     weights(2)
-    give_core(0)
+    rs_core(1)
     spread_back(2)
-    step1(0)
+    rs_axis(1)
     back(1)
     weights(1)
-    give_core(1)
-    for u in PIECES[0]:
-        step2(u)
+    rs_core(2)
+    each(rs_plane, 0)
     spread_back(1)
-    step1(1)
+    rs_axis(2)
     back(0)
     weights(0)
-    for u in PIECES[0]:
-        step3(u)
+    rs_core(3)
+    each(rs_plane, 1)
     spread_back(0)
-    for u in PIECES[1]:
-        step2(u)
-    squares = jnp.zeros((), F32)
+    rs_axis(3)
     dx0 = (up[4:20] * in_tile).astype(BF16).reshape(8, 2, WIDE, 256)
     mt = mean[3:11].reshape(512, 128).T.astype(BF16)
     ge = nn(mt[0:64], dx0[:, 0].reshape(512, 256)) + nn(mt[64:128], dx0[:, 1].reshape(512, 256))
     for e in range(2):
         grad[e, 31] = jnp.zeros((256, 128), BF16)
         grad[e, 31, 0:64, :] = ge[:, e * 128 : (e + 1) * 128].astype(BF16)
-    give_core(2)
-    for u in PIECES[0]:
-        squares = squares + step4(u)
-    step1(2)
-    for u in PIECES[1]:
-        step3(u)
-    for u in PIECES[2]:
-        step2(u)
-    for u in PIECES[1]:
-        squares = squares + step4(u)
-    for u in PIECES[2]:
-        step3(u)
-    for u in PIECES[2]:
-        squares = squares + step4(u)
-
-    p1, rows = own_rows(2, 3)
-    full = jnp.full((8, 128), squares, F32)
-    high = full.astype(BF16).astype(F32)
-    gath[core, p1, 8, rows, :] = jnp.concatenate([high, full - high], 0).astype(BF16)
-
-    for level in (3, 2, 1):
-        for g in range(3):
-            axis = (g + level - 1) % 3
-            if level < 3:
-                for k in (1, 2, 3):
-                    copies["g", level + 1, g, k].wait_recv()
-            p1, rows = own_rows(g, level)
-            part = gath.at[core, p1, pl.ds(3 * g, 3), rows, :]
-            for k in (1, 2, 3):
-                send(("g", level, g, k), part, part, at(axis, k), ag, g * 9 + (3 - level) * 3 + k - 1)
-    for g in range(3):
-        part = gath.at[core, pos[g], pl.ds(3 * g, 3)]
-        send(("h", g, 0), part, part, other, ag, 27 + g * 4)
-    for k in (1, 2, 3):
-        for g in range(3):
-            copies["g", 1, g, k].wait_recv()
-            part = gath.at[core, lax.rem(pos[g] + 4 - k, 4), pl.ds(3 * g, 3)]
-            send(("h", g, k), part, part, other, ag, 27 + g * 4 + k)
-    for g in range(3):
-        for k in range(4):
-            copies["h", g, k].wait_recv()
-
-    stats = jnp.zeros((1, 128), F32)
-    for e in range(2):
-        for p in range(4):
-            stats = stats + jnp.sum(gath[e, p, 8].astype(F32), axis=0, keepdims=True)
-    entries = 31 * 65536 + 16384
-    scale_ref[...] = jnp.broadcast_to(1.0 / jnp.sqrt(stats / (8.0 * entries) + 1e-06), (8, 128))
+    rs_core(4)
+    each(ag_plane, 0)
+    rs_axis(4)
+    each(rs_plane, 2)
+    each(ag_plane, 1)
+    each(rs_plane, 3)
+    each(ag_axis, 0)
+    each(rs_plane, 4)
+    each(ag_plane, 2)
+    each(ag_axis, 1)
+    each(ag_plane, 3)
+    each(ag_plane, 4)
+    each(ag_axis, 2)
+    each(ag_core, 0)
+    each(ag_axis, 3)
+    each(ag_axis, 4)
+    squares = square(0)
+    each(ag_core, 1)
     for c in lat_copies + lon_copies + cot_copies + mean_copies:
         c.wait_send()
-    for c in copies.values():
-        c.wait_send()
+    sent("cab")
+    squares = squares + square(1) + square(2)
+    each(ag_core, 2)
+    sent("p")
+    squares = squares + square(3) + square(4)
+    each(ag_core, 3)
+    squares = squares + square(5) + square(6)
+    each(ag_core, 4)
+    sent("g")
+    squares = squares + square(7)
+    entries = 31 * 65536 + 16384
+    squares = jnp.sum(jnp.sum(squares, axis=0, keepdims=True), axis=1, keepdims=True)
+    scale_ref[...] = jnp.broadcast_to(1.0 / jnp.sqrt(squares / entries + 1e-06), (8, 128))
+    sent("h")
+    for c in stores:
+        c.wait()
 
 
 def finish(gath_hbm, coarse_hbm, scale_ref, coarse_out, kup_out, dup_out, eup_out, gin, kup, dup, eup, in_s, out_s):
@@ -465,7 +452,7 @@
     through.start()
     reads = []
     for u in range(8):
-        c = pltpu.make_async_copy(gath_hbm.at[:, :, PLACE[u]], gin.at[u], in_s.at[u])
+        c = pltpu.make_async_copy(gath_hbm.at[u], gin.at[u], in_s.at[u])
         c.start()
         reads.append(c)
     scale = scale_ref[0:1, :]
@@ -494,9 +481,11 @@
                 write(dup, dup_out, 1)
             elif block == 31:
                 write(eup, eup_out, 2)
-            elif (block - 4) % 9 == 8:
-                l = 2 - (block - 4) // 9
-                write(kup.at[pl.ds(9 * l, 9)], kup_out.at[pl.ds(9 * l, 9)], 3 + l)
+            elif block >= 4 and ((block - 4) % 9 == 8 or block % 4 == 3 or block == 30):
+                since = max(4 * u, block - (block - 4) % 9)
+                n = block - since + 1
+                at = 9 * (2 - (block - 4) // 9) + (since - 4) % 9
+                write(kup.at[pl.ds(at, n)], kup_out.at[pl.ds(at, n)], len(writes) + 2)
     for c in writes:
         c.wait()
 
@@ -508,11 +497,11 @@
         body,
         out_shape=(
             jax.ShapeDtypeStruct((8, 24, 256), BF16),
-            jax.ShapeDtypeStruct((2, 4, 9, 256, 128), BF16),
+            jax.ShapeDtypeStruct((8, 2, 4, 256, 128), BF16),
             jax.ShapeDtypeStruct((8, 128), F32),
         ),
         in_specs=[vmem, vmem, vmem, vmem, hbm, hbm, vmem],
-        out_specs=(vmem,) * 3,
+        out_specs=(vmem, hbm, vmem),
         scratch_shapes=[
             pltpu.VMEM((3, 3, 3, 256, 256), BF16),
             pltpu.VMEM((2, 2, 256, 256), BF16),
@@ -540,9 +529,8 @@
             pltpu.VMEM((32, 256, 128), BF16),
             pltpu.VMEM((8, 3, 256, 128), BF16),
             pltpu.VMEM((8, 256, 128), BF16),
-            pltpu.VMEM((8, 3, 64, 128), BF16),
-            pltpu.VMEM((8, 64, 128), BF16),
-            pltpu.VMEM((8, 3, 16, 128), BF16),
+            pltpu.VMEM((8, 15, 16, 128), BF16),
+            pltpu.VMEM((8, 2, 4, 256, 128), BF16),
             pltpu.SemaphoreType.DMA((2,)),
             pltpu.SemaphoreType.DMA((7,)),
             pltpu.SemaphoreType.DMA((7,)),
@@ -550,15 +538,14 @@
             pltpu.SemaphoreType.DMA((15,)),
             pltpu.SemaphoreType.DMA((2, 8)),
             pltpu.SemaphoreType.DMA((2, 8)),
-            pltpu.SemaphoreType.DMA((75,)),
-            pltpu.SemaphoreType.DMA((75,)),
-            pltpu.SemaphoreType.DMA((39,)),
-            pltpu.SemaphoreType.DMA((39,)),
+            pltpu.SemaphoreType.DMA((301,)),
+            pltpu.SemaphoreType.DMA((301,)),
+            pltpu.SemaphoreType.DMA((8,)),
         ],
         compiler_params=pltpu.CompilerParams(
             collective_id=0, has_side_effects=True, vmem_limit_bytes=60 * 1024 * 1024
         ),
-    )(records.reshape(128, 1024), cell_ids.reshape(128, 16), counts, embed, kernels, down, cotangent)
+    )(records.reshape(128, 1024), jnp.swapaxes(cell_ids, 1, 2).reshape(16, 128), counts, embed, kernels, down, cotangent)
     coarse, kup, dup, eup = pl.pallas_call(
         finish,
         out_shape=(
@@ -575,9 +562,9 @@
             pltpu.VMEM((4, 256, 256), BF16),
             pltpu.VMEM((64, 256), BF16),
             pltpu.SemaphoreType.DMA((8,)),
-            pltpu.SemaphoreType.DMA((6,)),
+            pltpu.SemaphoreType.DMA((16,)),
         ],
-        compiler_params=pltpu.CompilerParams(vmem_limit_bytes=24 * 1024 * 1024),
+        compiler_params=pltpu.CompilerParams(vmem_limit_bytes=60 * 1024 * 1024),
     )(gath, coarse, scale)
     return coarse, kup.reshape(3, 3, 3, 256, 256), dup.reshape(2, 2, 256, 256), eup
 

time: 105 us -> 91.5 us (0.87)
  Pallas kernels: 99.1 us -> 90.5 us
  local copies, waits for them, and re-layouts: 5.32 us -> 0 us
    pallas_call x1, Pallas kernels: 96.5 us -> 85.5 us  [on_device(): pl.pallas_call(body, out_shape=(jax.ShapeDtypeStruct((8, 24, 256), BF16),...]
    unnamed x7 -> x0, local copies, waits for them, and re-layouts: 5.32 us -> none
    pallas_call x1, Pallas kernels: 2.54 us -> 4.98 us  [on_device(): pl.pallas_call(finish, out_shape=(jax.ShapeDtypeStruct((8, 24, 256), BF16...]
where the time goes in v2:
time: 91.5 us; the launch traced here: 91.3 us
  Pallas kernels  90.5 us (99%)
    pallas_call x1, Pallas kernels, on_device(): pl.pallas_call(body, out_shape=(jax.ShapeDtypeStruct((8, 24, 256), BF16),...  85.5 us
    pallas_call x1, Pallas kernels, on_device(): pl.pallas_call(finish, out_shape=(jax.ShapeDtypeStruct((8, 24, 256), BF16...  4.98 us

profile of v2, /device:TPU:1, one launch (start us, length us, event | category | flops | bytes accessed | tf_op | source)
XLA Modules:
  0.0 91.3 jit_solution(17424100408695122317)
XLA Ops:
  0.6 85.5 %shard_map.102 = (bf16[8,24,256]{2,1,0:T(8,128)(2,1)}, bf16[8,2,4,256,128]{4,3,2,1,0:T(8,128)(2,1)}, f32[8,128]{1,0:T(8,128)}) custom-call(bf16[128,1024]{1,0:T(8,128)(2,1)} %bitcast.6, s32[16,128]{1,0:T(8,128)} %bitcast.7, s32[1,128]{1,0:T(1,128)} %counts_ref.1, bf16[64,256]{1,0:T(8,128)(2,1)} %embed_ref.1, bf16[3,3,3,256,256]{4,3,2,1,0:T(8,128)(2,1)} %kern_hbm.1, ...), custom_call_target="tpu_custom_call" | custom-call | tf_op jit(solution)/shard_map/pallas_call | solution.py:496
  86.1 5.0 %shard_map.103 = (bf16[8,24,256]{2,1,0:T(8,128)(2,1)}, bf16[27,256,256]{2,1,0:T(8,128)(2,1)}, bf16[4,256,256]{2,1,0:T(8,128)(2,1)}, bf16[64,256]{1,0:T(8,128)(2,1)}) custom-call(bf16[8,2,4,256,128]{4,3,2,1,0:T(8,128)(2,1)} %get-tuple-element.11.gath_hbm, bf16[8,24,256]{2,1,0:T(8,128)(2,1)} %get-tuple-element.12.coarse_hbm, f32[8,128]{1,0:T(8,128)} %get-tuple-element.13.scale_ref), custom_call_target="tpu_custom_call" | custom-call | tf_op jit(solution)/shard_map/pallas_call | solution.py:549

commit v3 on v2

--- a/solution.py
+++ b/solution.py
@@ -23,19 +23,23 @@
 
 
 def body(
-    records_ref, ids_ref, counts_ref, embed_ref, kern_hbm, down_hbm, cot_ref,
+    records_hbm, ids_ref, counts_ref, embed_ref, kern_hbm, down_hbm, cot_hbm,
     coarse_ref, gath_hbm, scale_ref,
-    kern_ref, down_ref, table, arr1, out2, in2,
+    kern_ref, down_ref, cot_ref, table, arr1, out2, in2,
     onehot, spread, mean, cpad, fine_e, fine_o, eo, up, x3, fac, dy3, dym, xt, xl, ybuf,
     grad, core_in, acc1, in1, acc2, in2r, gath,
     load_s, d1_s, d1_r, d2_s, d2_r, halo_s, halo_r, sum_s, sum_r, out_s,
 ):
+    early = [
+        pltpu.make_async_copy(records_hbm, table.at[:, :, pl.ds(0, 1024)], load_s.at[2]),
+        pltpu.make_async_copy(cot_hbm, cot_ref, load_s.at[3]),
+    ]
+    for c in early:
+        c.start()
     loads = [
         pltpu.make_async_copy(kern_hbm, kern_ref, load_s.at[0]),
         pltpu.make_async_copy(down_hbm, down_ref, load_s.at[1]),
     ]
-    for c in loads:
-        c.start()
     lat = lax.axis_index("lat")
     lon = lax.axis_index("lon")
     xx = lax.rem(lon // 2, 2) * 2 + lat // 4
@@ -77,7 +81,10 @@
     digits = nn(jnp.where(ll == lane, 1.0, 0.0).astype(BF16), (cell >> 5).astype(F32).astype(BF16))
     digits = digits + nn(jnp.where(ll == lane + 8, 1.0, 0.0).astype(BF16), (cell & 31).astype(F32).astype(BF16))
     digits = digits.T
-    table[:, :, 0:1024] = records_ref[...].reshape(8, 16, 1024)
+    for c in loads:
+        c.start()
+    for c in early:
+        c.wait()
     table[:, :, 1024:1152] = digits.astype(BF16).reshape(8, 16, 128)
     cpad[2:10, 8:32, :] = cot_ref[...].astype(F32)
     pl.semaphore_wait(barrier, len(partners))
@@ -248,86 +255,102 @@
             else:
                 xl[start : start + half] = (x * in_tile).astype(BF16)
 
-    sum0 = jnp.zeros((512, 256), F32)
-    sum1 = jnp.zeros((512, 256), F32)
     last = xl[6:22].reshape(8, 2, WIDE, 256)
     rights = eo[2:10].reshape(512, 512)
     for a in range(2):
-        piece = last[:, a].reshape(512, 256)
-        sum0 = sum0 + nn(piece, down_ref[a, 0])
-        sum1 = sum1 + nn(piece, down_ref[a, 1])
-        g = nn(piece.T, rights).astype(BF16)
+        g = nn(last[:, a].reshape(512, 256).T, rights).astype(BF16)
         for b in range(2):
             for e in range(2):
                 grad[e, 2 * a + b] = g[:, b * 256 + e * 128 : b * 256 + (e + 1) * 128]
-    total = sum0 + pltpu.roll(sum1, 511, 0)
-    for h in range(2):
-        ybuf[h] = total[:, h * 128 : (h + 1) * 128]
-    for h in range(2):
-        picked = ybuf[h, pl.ds(0, 256, stride=2), :].reshape(8, 32, 128)
-        coarse_ref[:, :, h * 128 : (h + 1) * 128] = picked[:, 4:28].astype(BF16)
-
-    copies = {}
+
+    def downsample():
+        sum0 = jnp.zeros((512, 256), F32)
+        sum1 = jnp.zeros((512, 256), F32)
+        last = xl[6:22].reshape(8, 2, WIDE, 256)
+        for a in range(2):
+            piece = last[:, a].reshape(512, 256)
+            sum0 = sum0 + nn(piece, down_ref[a, 0])
+            sum1 = sum1 + nn(piece, down_ref[a, 1])
+        total = sum0 + pltpu.roll(sum1, 511, 0)
+        for h in range(2):
+            ybuf[h] = total[:, h * 128 : (h + 1) * 128]
+        for h in range(2):
+            picked = ybuf[h, pl.ds(0, 256, stride=2), :].reshape(8, 32, 128)
+            coarse_ref[:, :, h * 128 : (h + 1) * 128] = picked[:, 4:28].astype(BF16)
+
     stores = []
-
-    def send(key, src, dst, who, index):
-        copies[key] = remote(src, dst, sum_s.at[index], sum_r.at[index], who)
+    owed = []
+
+    def stage(kind, u):
+        index = "abpgh".index(kind) * 8 + u
+        return sum_s.at[index], sum_r.at[index]
+
+    def arrive(sem, like):
+        pltpu.make_async_copy(like, like, sem).wait()
 
     def rs_core(piece):
         b0, n = 4 * PIECES[piece][0], 4 * len(PIECES[piece])
-        send(("c", piece), grad.at[1 - core, pl.ds(b0, n)], core_in.at[pl.ds(b0, n)], other, 37 * 8 + piece)
+        blocks = core_in.at[pl.ds(b0, n)]
+        remote(grad.at[1 - core, pl.ds(b0, n)], blocks, sum_s.at[40 + piece], sum_r.at[40 + piece], other)
+        owed.append((sum_s.at[40 + piece], blocks))
 
     def rs_axis(piece):
-        copies["c", piece].wait_recv()
+        arrive(sum_r.at[40 + piece], core_in.at[pl.ds(4 * PIECES[piece][0], 4 * len(PIECES[piece]))])
         for u in PIECES[piece]:
             for p in range(4):
                 acc1[4 * u + p] = (grad[core, 4 * u + p].astype(F32) + core_in[4 * u + p].astype(F32)).astype(BF16)
+            out, into = stage("a", u)
             for k in (1, 2, 3):
                 p = lax.rem(pos[u % 3] + k, 4)
-                send(("a", u, k), acc1.at[4 * u + p], in1.at[u, k - 1], along(u % 3, k), u * 37 + k - 1)
+                remote(acc1.at[4 * u + p], in1.at[u, k - 1], out, into, along(u % 3, k))
+            owed.append((out, in1.at[u]))
 
     def rs_plane(u):
         axis = u % 3
-        for k in (1, 2, 3):
-            copies["a", u, k].wait_recv()
+        arrive(stage("a", u)[1], in1.at[u])
         s = acc1[4 * u + pos[axis]].astype(F32)
         for k in range(3):
             s = s + in1[u, k].astype(F32)
         acc2[u] = s.astype(BF16)
+        out, into = stage("b", u)
         for i, (kb, kc) in enumerate(PLANE):
             row = lax.rem(pos[(axis + 1) % 3] + kb, 4) * 64 + lax.rem(pos[(axis + 2) % 3] + kc, 4) * 16
             src = acc2.at[u, pl.ds(pl.multiple_of(row, 16), 16)]
-            send(("b", u, i), src, in2r.at[u, i], across(axis, kb, kc), u * 37 + 3 + i)
+            remote(src, in2r.at[u, i], out, into, across(axis, kb, kc))
+        owed.append((out, in2r.at[u]))
 
     def ag_plane(u):
         axis = u % 3
-        for i in range(15):
-            copies["b", u, i].wait_recv()
+        arrive(stage("b", u)[1], in2r.at[u])
         rows = pl.ds(pl.multiple_of(pos[(axis + 1) % 3] * 64 + pos[(axis + 2) % 3] * 16, 16), 16)
         s = acc2[u, rows, :].astype(F32)
         for i in range(15):
             s = s + in2r[u, i].astype(F32)
         part = gath.at[u, core, pos[axis], rows, :]
         gath[u, core, pos[axis], rows, :] = s.astype(BF16)
-        for i, (kb, kc) in enumerate(PLANE):
-            send(("p", u, i), part, part, across(axis, kb, kc), u * 37 + 18 + i)
+        out, into = stage("p", u)
+        for kb, kc in PLANE:
+            remote(part, part, out, into, across(axis, kb, kc))
+        owed.append((out, in2r.at[u]))
 
     def ag_axis(u):
         axis = u % 3
-        for i in range(15):
-            copies["p", u, i].wait_recv()
+        arrive(stage("p", u)[1], in2r.at[u])
         part = gath.at[u, core, pos[axis]]
+        out, into = stage("g", u)
         for k in (1, 2, 3):
-            send(("g", u, k), part, part, along(axis, k), u * 37 + 33 + k - 1)
+            remote(part, part, out, into, along(axis, k))
+        owed.append((out, in1.at[u]))
 
     def ag_core(u):
-        for k in (1, 2, 3):
-            copies["g", u, k].wait_recv()
+        arrive(stage("g", u)[1], in1.at[u])
         part = gath.at[u, core]
-        send(("h", u), part, part, other, u * 37 + 36)
+        out, into = stage("h", u)
+        remote(part, part, out, into, other)
+        owed.append((out, part))
 
     def square(u):
-        copies["h", u].wait_recv()
+        arrive(stage("h", u)[1], gath.at[u, core])
         c = pltpu.make_async_copy(gath.at[u], gath_hbm.at[u], out_s.at[u])
         c.start()
         stores.append(c)
@@ -380,9 +403,9 @@
         for u in PIECES[piece]:
             step(u)
 
-    def sent(kinds):
-        for key in [key for key in copies if key[0] in kinds]:
-            copies.pop(key).wait_send()
+    def sent(keep):
+        while len(owed) > keep:
+            arrive(*owed.pop(0))
 
     rs_core(0)
     back(2)
@@ -412,6 +435,7 @@
     rs_core(4)
     each(ag_plane, 0)
     rs_axis(4)
+    downsample()
     each(rs_plane, 2)
     each(ag_plane, 1)
     each(rs_plane, 3)
@@ -429,20 +453,20 @@
     each(ag_core, 1)
     for c in lat_copies + lon_copies + cot_copies + mean_copies:
         c.wait_send()
-    sent("cab")
+    sent(24)
     squares = squares + square(1) + square(2)
     each(ag_core, 2)
-    sent("p")
+    sent(12)
     squares = squares + square(3) + square(4)
     each(ag_core, 3)
     squares = squares + square(5) + square(6)
     each(ag_core, 4)
-    sent("g")
+    sent(1)
     squares = squares + square(7)
     entries = 31 * 65536 + 16384
     squares = jnp.sum(jnp.sum(squares, axis=0, keepdims=True), axis=1, keepdims=True)
     scale_ref[...] = jnp.broadcast_to(1.0 / jnp.sqrt(squares / entries + 1e-06), (8, 128))
-    sent("h")
+    sent(0)
     for c in stores:
         c.wait()
 
@@ -500,11 +524,12 @@
             jax.ShapeDtypeStruct((8, 2, 4, 256, 128), BF16),
             jax.ShapeDtypeStruct((8, 128), F32),
         ),
-        in_specs=[vmem, vmem, vmem, vmem, hbm, hbm, vmem],
+        in_specs=[hbm, vmem, vmem, vmem, hbm, hbm, hbm],
         out_specs=(vmem, hbm, vmem),
         scratch_shapes=[
             pltpu.VMEM((3, 3, 3, 256, 256), BF16),
             pltpu.VMEM((2, 2, 256, 256), BF16),
+            pltpu.VMEM((8, 24, 256), BF16),
             pltpu.VMEM((8, 16, 1152), BF16),
             pltpu.VMEM((8, 16, 1152), BF16),
             pltpu.VMEM((16, 16, 640), BF16),
@@ -531,21 +556,21 @@
             pltpu.VMEM((8, 256, 128), BF16),
             pltpu.VMEM((8, 15, 16, 128), BF16),
             pltpu.VMEM((8, 2, 4, 256, 128), BF16),
-            pltpu.SemaphoreType.DMA((2,)),
+            pltpu.SemaphoreType.DMA((4,)),
             pltpu.SemaphoreType.DMA((7,)),
             pltpu.SemaphoreType.DMA((7,)),
             pltpu.SemaphoreType.DMA((15,)),
             pltpu.SemaphoreType.DMA((15,)),
             pltpu.SemaphoreType.DMA((2, 8)),
             pltpu.SemaphoreType.DMA((2, 8)),
-            pltpu.SemaphoreType.DMA((301,)),
-            pltpu.SemaphoreType.DMA((301,)),
+            pltpu.SemaphoreType.DMA((45,)),
+            pltpu.SemaphoreType.DMA((45,)),
             pltpu.SemaphoreType.DMA((8,)),
         ],
         compiler_params=pltpu.CompilerParams(
             collective_id=0, has_side_effects=True, vmem_limit_bytes=60 * 1024 * 1024
         ),
-    )(records.reshape(128, 1024), jnp.swapaxes(cell_ids, 1, 2).reshape(16, 128), counts, embed, kernels, down, cotangent)
+    )(records.reshape(8, 16, 1024), jnp.swapaxes(cell_ids, 1, 2).reshape(16, 128), counts, embed, kernels, down, cotangent)
     coarse, kup, dup, eup = pl.pallas_call(
         finish,
         out_shape=(

time: 91.5 us -> 86.4 us (0.944)
  Pallas kernels: 90.5 us -> 85.4 us
    pallas_call x1, Pallas kernels: 85.5 us -> 80.4 us  [on_device(): pl.pallas_call(body, out_shape=(jax.ShapeDtypeStruct((8, 24, 256), BF16),...]
where the time goes in v3:
time: 86.4 us; the launch traced here: 86.2 us
  Pallas kernels  85.4 us (99%)
    pallas_call x1, Pallas kernels, on_device(): pl.pallas_call(body, out_shape=(jax.ShapeDtypeStruct((8, 24, 256), BF16),...  80.4 us
    pallas_call x1, Pallas kernels, on_device(): pl.pallas_call(finish, out_shape=(jax.ShapeDtypeStruct((8, 24, 256), BF16...  4.98 us

profile of v3, /device:TPU:1, one launch (start us, length us, event | category | flops | bytes accessed | tf_op | source)
XLA Modules:
  0.0 86.2 jit_solution(14819642893632332506)
XLA Ops:
  0.6 80.4 %shard_map.102 = (bf16[8,24,256]{2,1,0:T(8,128)(2,1)}, bf16[8,2,4,256,128]{4,3,2,1,0:T(8,128)(2,1)}, f32[8,128]{1,0:T(8,128)}) custom-call(bf16[8,16,1024]{2,1,0:T(8,128)(2,1)} %bitcast.6, s32[16,128]{1,0:T(8,128)} %bitcast.7, s32[1,128]{1,0:T(1,128)} %counts_ref.1, bf16[64,256]{1,0:T(8,128)(2,1)} %embed_ref.1, bf16[3,3,3,256,256]{4,3,2,1,0:T(8,128)(2,1)} %kern_hbm.1, ...), custom_call_target="tpu_custom_call" | custom-call | tf_op jit(solution)/shard_map/pallas_call | solution.py:520
  81.1 5.0 %shard_map.103 = (bf16[8,24,256]{2,1,0:T(8,128)(2,1)}, bf16[27,256,256]{2,1,0:T(8,128)(2,1)}, bf16[4,256,256]{2,1,0:T(8,128)(2,1)}, bf16[64,256]{1,0:T(8,128)(2,1)}) custom-call(bf16[8,2,4,256,128]{4,3,2,1,0:T(8,128)(2,1)} %get-tuple-element.11.gath_hbm, bf16[8,24,256]{2,1,0:T(8,128)(2,1)} %get-tuple-element.12.coarse_hbm, f32[8,128]{1,0:T(8,128)} %get-tuple-element.13.scale_ref), custom_call_target="tpu_custom_call" | custom-call | tf_op jit(solution)/shard_map/pallas_call | solution.py:574

commit v4 on v3

--- a/solution.py
+++ b/solution.py
@@ -28,7 +28,7 @@
     kern_ref, down_ref, cot_ref, table, arr1, out2, in2,
     onehot, spread, mean, cpad, fine_e, fine_o, eo, up, x3, fac, dy3, dym, xt, xl, ybuf,
     grad, core_in, acc1, in1, acc2, in2r, gath,
-    load_s, d1_s, d1_r, d2_s, d2_r, halo_s, halo_r, sum_s, sum_r, out_s,
+    load_s, d_s, d_r, halo_s, halo_r, sum_s, sum_r, out_s,
 ):
     early = [
         pltpu.make_async_copy(records_hbm, table.at[:, :, pl.ds(0, 1024)], load_s.at[2]),
@@ -96,13 +96,14 @@
         c.start()
         return c
 
-    lat_copies = []
+    def arrive(sem, like):
+        pltpu.make_async_copy(like, like, sem).wait()
+
     for k in range(1, 8):
         p = lax.rem(lat + k, 8)
-        lat_copies.append(remote(table.at[p], arr1.at[lat], d1_s.at[k - 1], d1_r.at[k - 1], (p, lon)))
+        remote(table.at[p], arr1.at[lat], d_s.at[0], d_r.at[0], (p, lon))
     arr1[lat] = table[lat]
-    for c in lat_copies:
-        c.wait_recv()
+    arrive(d_r.at[0], arr1.at[pl.ds(0, 7)])
     flat = arr1[...].reshape(128, 1152)
     rho = lax.broadcasted_iota(jnp.int32, (256, 128), 0)
     came = lax.broadcasted_iota(jnp.int32, (256, 128), 1)
@@ -113,10 +114,9 @@
     moved_ids = nn(halves[0], flat[:, 1024:1152]) + nn(halves[1], second)
     out2[:, :, 0:512] = moved.astype(BF16).reshape(16, 16, 512)
     out2[:, :, 512:640] = moved_ids.astype(BF16).reshape(16, 16, 128)
-    lon_copies = []
     for k in range(1, 16):
         q = lax.rem(lon + k, 16)
-        lon_copies.append(remote(out2.at[q], in2.at[lon], d2_s.at[k - 1], d2_r.at[k - 1], (lat, q)))
+        remote(out2.at[q], in2.at[lon], d_s.at[1], d_r.at[1], (lat, q))
     in2[lon] = out2[lon]
 
     def span(step, rows, lead, cols, near):
@@ -154,8 +154,7 @@
 
     cot_copies = halo(cpad, 8, 2, 24, 0)
 
-    for c in lon_copies:
-        c.wait_recv()
+    arrive(d_r.at[1], in2.at[pl.ds(0, 15)])
     code = in2[:, :, 512:640].reshape(256, 128).astype(F32)
     code = code * 32.0 + pltpu.roll(code, 120, 1)
     odds = (((code.astype(jnp.int32) * 1366) >> 16) & 1).astype(F32)
@@ -284,9 +283,6 @@
     def stage(kind, u):
         index = "abpgh".index(kind) * 8 + u
         return sum_s.at[index], sum_r.at[index]
-
-    def arrive(sem, like):
-        pltpu.make_async_copy(like, like, sem).wait()
 
     def rs_core(piece):
         b0, n = 4 * PIECES[piece][0], 4 * len(PIECES[piece])
@@ -451,7 +447,9 @@
     each(ag_axis, 4)
     squares = square(0)
     each(ag_core, 1)
-    for c in lat_copies + lon_copies + cot_copies + mean_copies:
+    arrive(d_s.at[0], arr1.at[pl.ds(0, 7)])
+    arrive(d_s.at[1], in2.at[pl.ds(0, 15)])
+    for c in cot_copies + mean_copies:
         c.wait_send()
     sent(24)
     squares = squares + square(1) + square(2)
@@ -557,10 +555,8 @@
             pltpu.VMEM((8, 15, 16, 128), BF16),
             pltpu.VMEM((8, 2, 4, 256, 128), BF16),
             pltpu.SemaphoreType.DMA((4,)),
-            pltpu.SemaphoreType.DMA((7,)),
-            pltpu.SemaphoreType.DMA((7,)),
-            pltpu.SemaphoreType.DMA((15,)),
-            pltpu.SemaphoreType.DMA((15,)),
+            pltpu.SemaphoreType.DMA((2,)),
+            pltpu.SemaphoreType.DMA((2,)),
             pltpu.SemaphoreType.DMA((2, 8)),
             pltpu.SemaphoreType.DMA((2, 8)),
             pltpu.SemaphoreType.DMA((45,)),

time: 86.4 us -> 86 us (level)
  no operation moved by 1% of the time
where the time goes in v4:
time: 86 us; the launch traced here: 85.8 us
  Pallas kernels  85 us (99%)
    pallas_call x1, Pallas kernels, on_device(): pl.pallas_call(body, out_shape=(jax.ShapeDtypeStruct((8, 24, 256), BF16),...  80 us
    pallas_call x1, Pallas kernels, on_device(): pl.pallas_call(finish, out_shape=(jax.ShapeDtypeStruct((8, 24, 256), BF16...  4.98 us

profile of v4, /device:TPU:1, one launch (start us, length us, event | category | flops | bytes accessed | tf_op | source)
XLA Modules:
  0.0 85.8 jit_solution(4502483932134252599)
XLA Ops:
  0.6 80.0 %shard_map.102 = (bf16[8,24,256]{2,1,0:T(8,128)(2,1)}, bf16[8,2,4,256,128]{4,3,2,1,0:T(8,128)(2,1)}, f32[8,128]{1,0:T(8,128)}) custom-call(bf16[8,16,1024]{2,1,0:T(8,128)(2,1)} %bitcast.6, s32[16,128]{1,0:T(8,128)} %bitcast.7, s32[1,128]{1,0:T(1,128)} %counts_ref.1, bf16[64,256]{1,0:T(8,128)(2,1)} %embed_ref.1, bf16[3,3,3,256,256]{4,3,2,1,0:T(8,128)(2,1)} %kern_hbm.1, ...), custom_call_target="tpu_custom_call" | custom-call | tf_op jit(solution)/shard_map/pallas_call | solution.py:518
  80.7 5.0 %shard_map.103 = (bf16[8,24,256]{2,1,0:T(8,128)(2,1)}, bf16[27,256,256]{2,1,0:T(8,128)(2,1)}, bf16[4,256,256]{2,1,0:T(8,128)(2,1)}, bf16[64,256]{1,0:T(8,128)(2,1)}) custom-call(bf16[8,2,4,256,128]{4,3,2,1,0:T(8,128)(2,1)} %get-tuple-element.11.gath_hbm, bf16[8,24,256]{2,1,0:T(8,128)(2,1)} %get-tuple-element.12.coarse_hbm, f32[8,128]{1,0:T(8,128)} %get-tuple-element.13.scale_ref), custom_call_target="tpu_custom_call" | custom-call | tf_op jit(solution)/shard_map/pallas_call | solution.py:570
